TPU v7x, 128 devices: a whole 4x4x4 slice. The times are simulated.
128 devices in a mesh: tm: 16 (over y, x_hi, core), space: 8 (over x_lo, z).
Axes of the slice: x: 4 (x_hi: 2, x_lo: 2; x = x_hi * 2 + x_lo), y: 4, z: 4, core: 2. Of those that a mesh axis runs over, the one named last changes fastest.
Arguments:
- starts: float32 [16, 64, 128, 128], P('tm', 'space'), may hold values from -6 to 6
- diffusivity: float32 [64, 128, 128], P('space'), may hold values from 0.04 to 0.2
- velocity: float32 [2, 64, 128, 128], P(None, 'space'), may hold values from -0.1 to 0.1
- obstacle: int32 [64, 128, 128], P('space'), may hold values from 0 to 1, as said below
- substep_scale: float32 [12], replicated, may hold values from 0.5 to 1
- neighbors: int32 [64, 4], P('space'), may hold values from 0 to 64, as said below
- coarse_x: float32 [64, 64, 64], P('space'), may hold values from -1 to 1
- coarse_y: float32 [64, 128, 128], P('space'), may hold values from -1 to 1
Outputs:
- slice_ends: float32 [16, 64, 128, 128], P('tm', 'space')
- increment: float32 [16, 64, 128, 128], P('tm', 'space')
Inputs may be any that keep to these rules, and one draw needn't show every extreme that they name: `neighbors`: tiles form a grid of 8 by 8; each entry names the tile beside a tile in the given direction, or 64 on the grid's edge. The tiles 8 * k to 8 * (k + 1) - 1 fill grid row k, in any order within it, so a neighbour's number differs from the tile's block k by at most one block. `obstacle`: each tile holds one tube, a disc of radius 128 // 8 to 32 cells.
All inputs are finite; a program needn't handle non-finite values.
Results may differ from a plain program's by a relative error of at most 0.0002.
Values sent between devices are 32-bit elements; how exact they have to be, the bound alone decides.
A program may use at most 128 MiB of HBM per device.

v0:
```python
import jax
import jax.numpy as jnp
from jax import lax
from jax.sharding import PartitionSpec as P

SUB = 12


exact_precision = lax.Precision.HIGHEST


def padded(block, sides, width):
    for axis, dim in sides:
        count = lax.axis_size(axis)
        forward = [(i, i + 1) for i in range(count - 1)]
        backward = [(target, source) for source, target in forward]
        low = lax.ppermute(
            lax.slice_in_dim(block, block.shape[dim] - width, None, axis=dim), axis, forward
        )
        high = lax.ppermute(lax.slice_in_dim(block, 0, width, axis=dim), axis, backward)
        block = jnp.concatenate([low, block, high], axis=dim)
    return block


def picked(value, axis, root):
    return lax.dynamic_index_in_dim(lax.all_gather(value, axis), root, 0, keepdims=False)


def passed_along(block, axis, distance):
    devices = range(lax.axis_size(axis))
    route = [(i - distance, i) for i in devices if i - distance in devices]
    return lax.ppermute(block, axis, route)


def restrict(values):
    return 0.5 * (values[..., 0::2, :] + values[..., 1::2, :])


def prolong(coarse_values):
    return jnp.repeat(coarse_values, 2, axis=-2)


def apply_coarse(coarse_values, matrix_x, matrix_y):
    mixed_x = jnp.einsum("tij,...tjk->...tik", matrix_x, coarse_values, precision=exact_precision)
    return jnp.einsum("...tik,tlk->...til", mixed_x, matrix_y, precision=exact_precision)


def on_device(
    starts, diffusivity, velocity, obstacle, substep_scale, neighbors, coarse_x, coarse_y
):
    slice_count = starts.shape[0]
    tile_count = starts.shape[1]
    all_tiles = tile_count * lax.axis_size("space")
    block_base = lax.axis_index("space") * tile_count
    open_cells = 1.0 - obstacle.astype(jnp.float32)
    speed_x = velocity[0]
    speed_y = velocity[1]
    shifted = neighbors - block_base + tile_count
    lookup_index = jnp.where(neighbors == all_tiles, 3 * tile_count, shifted)

    def advance(substep_index, current):
        strength = substep_scale[substep_index]
        own_faces = jnp.stack(
            [current[:, :, 0, :], current[:, :, -1, :], current[:, :, :, 0], current[:, :, :, -1]],
            axis=2,
        )
        gathered = padded(own_faces, (("space", 1),), tile_count)
        gathered = jnp.concatenate([gathered, jnp.zeros_like(gathered[:, :1])], axis=1)
        west_face = gathered[:, lookup_index[:, 0], 1]
        east_face = gathered[:, lookup_index[:, 1], 0]
        south_face = gathered[:, lookup_index[:, 2], 3]
        north_face = gathered[:, lookup_index[:, 3], 2]
        from_west = jnp.concatenate([west_face[:, :, None, :], current[:, :, :-1, :]], axis=2)
        from_east = jnp.concatenate([current[:, :, 1:, :], east_face[:, :, None, :]], axis=2)
        from_south = jnp.concatenate([south_face[:, :, :, None], current[:, :, :, :-1]], axis=3)
        from_north = jnp.concatenate([current[:, :, :, 1:], north_face[:, :, :, None]], axis=3)
        laplace = from_west + from_east + from_south + from_north - 4.0 * current
        transport = speed_x * (from_east - from_west) + speed_y * (from_north - from_south)
        return open_cells * (current + strength * diffusivity * laplace - 0.5 * transport)

    fine_ends = lax.fori_loop(0, SUB, advance, starts)
    correction = fine_ends - prolong(apply_coarse(restrict(starts), coarse_x, coarse_y))
    coarse_jump = restrict(correction)
    first_coarse = picked(restrict(starts[0]), "tm", 0)
    every_jump = lax.all_gather(coarse_jump, "tm", axis=0, tiled=True)

    def sweep(state_now, jump):
        return (apply_coarse(state_now, coarse_x, coarse_y) + jump, state_now)

    last_state, history = lax.scan(sweep, first_coarse, every_jump)
    own_coarse = lax.dynamic_slice_in_dim(
        history, lax.axis_index("tm") * slice_count, slice_count, 0
    )
    slice_ends = prolong(apply_coarse(own_coarse, coarse_x, coarse_y)) + correction
    previous = passed_along(slice_ends[-1], "tm", 1)
    first_step = jnp.where(
        lax.axis_index("tm") == 0, jnp.zeros_like(previous), previous - starts[0]
    )
    increment = jnp.concatenate([first_step[None], slice_ends[:-1] - starts[1:]], axis=0)
    return (slice_ends, increment)


def solution(mesh):
    placed = (
        P("tm", "space", None, None),
        P("space", None, None),
        P(None, "space", None, None),
        P("space", None, None),
        P(),
        P("space", None),
        P("space", None, None),
        P("space", None, None),
    )
    return jax.shard_map(
        on_device,
        mesh=mesh,
        in_specs=placed,
        out_specs=(P("tm", "space", None, None), P("tm", "space", None, None)),
        check_vma=False,
    )
```

profile of v0, /device:TPU:27, one launch (start us, length us, event | category | flops | bytes accessed | tf_op | source)
XLA Modules:
  0.0 344.1 jit_solution(3638564841649857786)
XLA Ops:
  20.2 187.9 %while.25 = (s32[]{:T(128)}, f32[1,8,128,128]{2,1,3,0:T(8,128)S(1)}, f32[8,128,128]{1,0,2:T(8,128)}, f32[12]{0:T(128)S(1)}, f32[8,128,128]{1,0,2:T(8,128)}, /*in...) while((s32[]{:T(128)}, ...), condition=%wide.region_1.2_spmd, body=%wide.region_0.1_spmd.sunk | while | flops 2710714 | bytes 10800029 | solution.py:81
  20.5 5.6 %collective-permute-start = (f32[1,8,4,128]{3,2,1,0:T(4,128)S(1)}, f32[1,8,4,128]{3,2,1,0:T(4,128)S(1)}, u32[]{:S(2)}, u32[]{:S(2)}) collective-permute-start(f32[1,8,4,128]{3,2,1,0:T(4,128)S(1)} %pad_maximum_fusion.6), channel_id=1, source_target_pairs={{1,0},{2,1},{3,2},{4,3},{5,4},{6,5},{7,6},{9,8},{10,9},{11,10},{12... | collective-permute-start | bytes 49160 | tf_op jit(solution)/shard_map/while/body/eval_jaxpr/ppermute | solution.py:20
  29.9 2.9 collective-permute-done.1
  35.7 2.9 fusion.60
  41.6 2.7 collective-permute-start.1
  51.3 2.9 fusion.60
  57.0 2.9 collective-permute-start.1
  66.5 2.9 fusion.60
  72.4 2.7 collective-permute-start.1
  81.9 2.9 fusion.60
  87.8 2.7 collective-permute-start.1
  97.3 2.9 fusion.60
  103.2 2.7 collective-permute-start.1
  112.7 2.9 fusion.60
  118.6 2.7 collective-permute-start.1
  128.2 2.9 fusion.60
  134.0 2.7 collective-permute-start.1
  143.6 2.9 fusion.60
  149.4 2.7 collective-permute-start.1
  159.0 2.9 fusion.60
  162.2 2.6 collective-permute-start
  164.8 2.7 collective-permute-start.1
  174.4 2.9 fusion.60
  180.2 2.7 collective-permute-start.1
  189.8 2.9 fusion.60
  193.0 2.6 collective-permute-start
  195.6 2.7 collective-permute-start.1
  205.2 2.9 fusion.60
  214.3 58.7 %all-gather.4.cloned.1.call-done = f32[16,8,64,128]{3,2,1,0:T(8,128)} async-done(((f32[1,8,64,128]{3,2,1,0:T(8,128)}), f32[16,8,64,128]{3,2,1,0:T(8,128)}) %all-gather.4.cloned.1.call-update) | async-done | bytes 4194320 | tf_op jit(solution)/shard_map/all_gather | solution.py:85
  272.9 51.4 %while.26 = (s32[]{:T(128)}, f32[8,64,128]{2,1,0:T(8,128)S(1)}, f32[16,8,64,128]{3,2,1,0:T(8,128)}, f32[8,64,64]{2,1,0:T(8,128)S(1)}, f32[8,128,128]{2,1,0:T(8,128)S(1)}, /*index=5*/f32[16,8,64,128]{3,2,1,0:T(8,128)}, s32[]{:T(128)}) while((s32[]{:T(128)}, f32[8,64,128]{2,1,0:T(8,128)S(1)}, f32[16,8,64,128]{3,2,1,0:T(8,128)}, ...), condition=%wide.region_3.4_spmd, body=%wide.region_2.3_spmd.sunk | while | flops 151060480 | bytes 2490961 | solution.py:90
  327.1 3.2 collective-permute-start.2
  330.3 6.1 %collective-permute-done.2 = f32[8,128,128]{2,1,0:T(8,128)S(1)} collective-permute-done((f32[8,128,128]{2,1,0:T(8,128)S(1)}, f32[8,128,128]{2,1,0:T(8,128)S(1)}, u32[]{:S(2)}, u32[]{:S(2)}) %collective-permute-start.2) | collective-permute-done | bytes 524320 | tf_op jit(solution)/shard_map/ppermute | solution.py:32
  (322 shorter events, 181.4 us)
Async XLA Ops:
  7.2 206.1 %all-gather.6.cloned.1.call-start = ((), (), s32[]{:S(2)}) async-start(), calls=%async_computation.1 | async-start | bytes 4456448 | tf_op jit(solution)/shard_map/all_gather | solution.py:26
  7.2 9.9 %copy-start.5 = (s32[8,128,128]{2,1,0:T(8,128)S(1)}, s32[8,128,128]{2,1,0:T(8,128)}, u32[]{:S(2)}) copy-start(s32[8,128,128]{2,1,0:T(8,128)} %param.15) | copy-start | bytes 1572868
  10.2 262.7 %all-gather.4.cloned.1.call-start = ((), (), s32[]{:S(2)}) async-start(), calls=%async_computation | async-start | bytes 4456448 | tf_op jit(solution)/shard_map/all_gather | solution.py:85
  20.2 188.2 %copy-start.1 = (f32[8,64,64]{2,1,0:T(8,128)S(1)}, f32[8,64,64]{2,1,0:T(8,128)}, u32[]{:S(2)}) copy-start(f32[8,64,64]{2,1,0:T(8,128)} %param.18) | copy-start | bytes 393220
  20.5 9.3 %collective-permute-start = (f32[1,8,4,128]{3,2,1,0:T(4,128)S(1)}, f32[1,8,4,128]{3,2,1,0:T(4,128)S(1)}, u32[]{:S(2)}, u32[]{:S(2)}) collective-permute-start(f32[1,8,4,128]{3,2,1,0:T(4,128)S(1)} %pad_maximum_fusion.6), channel_id=1, source_target_pairs={{1,0},{2,1},{3,2},{4,3},{5,4},{6,5},{7,6},{9,8},{10,9},{11,10},{12... | collective-permute-start | bytes 49160 | tf_op jit(solution)/shard_map/while/body/eval_jaxpr/ppermute | solution.py:20
  26.2 6.6 %collective-permute-start.1 = (f32[1,8,4,128]{3,2,1,0:T(4,128)S(1)}, f32[1,8,4,128]{3,2,1,0:T(4,128)S(1)}, u32[]{:S(2)}, u32[]{:S(2)}) collective-permute-start(f32[1,8,4,128]{3,2,1,0:T(4,128)S(1)} %pad_maximum_fusion.6), channel_id=1, source_target_pairs={{0,1},{1,2},{2,3},{3,4},{4,5},{5,6},{6,7},{8,9},{9,10},{10,11},{11... | collective-permute-start | bytes 49160 | tf_op jit(solution)/shard_map/while/body/eval_jaxpr/ppermute | solution.py:17
  39.0 7.1 %collective-permute-start = (f32[1,8,4,128]{3,2,1,0:T(4,128)S(1)}, f32[1,8,4,128]{3,2,1,0:T(4,128)S(1)}, u32[]{:S(2)}, u32[]{:S(2)}) collective-permute-start(f32[1,8,4,128]{3,2,1,0:T(4,128)S(1)} %pad_maximum_fusion.6), channel_id=1, source_target_pairs={{1,0},{2,1},{3,2},{4,3},{5,4},{6,5},{7,6},{9,8},{10,9},{11,10},{12... | collective-permute-start | bytes 49160 | tf_op jit(solution)/shard_map/while/body/eval_jaxpr/ppermute | solution.py:20
  41.6 6.8 %collective-permute-start.1 = (f32[1,8,4,128]{3,2,1,0:T(4,128)S(1)}, f32[1,8,4,128]{3,2,1,0:T(4,128)S(1)}, u32[]{:S(2)}, u32[]{:S(2)}) collective-permute-start(f32[1,8,4,128]{3,2,1,0:T(4,128)S(1)} %pad_maximum_fusion.6), channel_id=1, source_target_pairs={{0,1},{1,2},{2,3},{3,4},{4,5},{5,6},{6,7},{8,9},{9,10},{10,11},{11... | collective-permute-start | bytes 49160 | tf_op jit(solution)/shard_map/while/body/eval_jaxpr/ppermute | solution.py:17
  54.6 7.1 %collective-permute-start = (f32[1,8,4,128]{3,2,1,0:T(4,128)S(1)}, f32[1,8,4,128]{3,2,1,0:T(4,128)S(1)}, u32[]{:S(2)}, u32[]{:S(2)}) collective-permute-start(f32[1,8,4,128]{3,2,1,0:T(4,128)S(1)} %pad_maximum_fusion.6), channel_id=1, source_target_pairs={{1,0},{2,1},{3,2},{4,3},{5,4},{6,5},{7,6},{9,8},{10,9},{11,10},{12... | collective-permute-start | bytes 49160 | tf_op jit(solution)/shard_map/while/body/eval_jaxpr/ppermute | solution.py:20
  57.0 6.6 %collective-permute-start.1 = (f32[1,8,4,128]{3,2,1,0:T(4,128)S(1)}, f32[1,8,4,128]{3,2,1,0:T(4,128)S(1)}, u32[]{:S(2)}, u32[]{:S(2)}) collective-permute-start(f32[1,8,4,128]{3,2,1,0:T(4,128)S(1)} %pad_maximum_fusion.6), channel_id=1, source_target_pairs={{0,1},{1,2},{2,3},{3,4},{4,5},{5,6},{6,7},{8,9},{9,10},{10,11},{11... | collective-permute-start | bytes 49160 | tf_op jit(solution)/shard_map/while/body/eval_jaxpr/ppermute | solution.py:17
  69.8 7.1 %collective-permute-start = (f32[1,8,4,128]{3,2,1,0:T(4,128)S(1)}, f32[1,8,4,128]{3,2,1,0:T(4,128)S(1)}, u32[]{:S(2)}, u32[]{:S(2)}) collective-permute-start(f32[1,8,4,128]{3,2,1,0:T(4,128)S(1)} %pad_maximum_fusion.6), channel_id=1, source_target_pairs={{1,0},{2,1},{3,2},{4,3},{5,4},{6,5},{7,6},{9,8},{10,9},{11,10},{12... | collective-permute-start | bytes 49160 | tf_op jit(solution)/shard_map/while/body/eval_jaxpr/ppermute | solution.py:20
  72.4 6.6 %collective-permute-start.1 = (f32[1,8,4,128]{3,2,1,0:T(4,128)S(1)}, f32[1,8,4,128]{3,2,1,0:T(4,128)S(1)}, u32[]{:S(2)}, u32[]{:S(2)}) collective-permute-start(f32[1,8,4,128]{3,2,1,0:T(4,128)S(1)} %pad_maximum_fusion.6), channel_id=1, source_target_pairs={{0,1},{1,2},{2,3},{3,4},{4,5},{5,6},{6,7},{8,9},{9,10},{10,11},{11... | collective-permute-start | bytes 49160 | tf_op jit(solution)/shard_map/while/body/eval_jaxpr/ppermute | solution.py:17
  85.2 7.1 %collective-permute-start = (f32[1,8,4,128]{3,2,1,0:T(4,128)S(1)}, f32[1,8,4,128]{3,2,1,0:T(4,128)S(1)}, u32[]{:S(2)}, u32[]{:S(2)}) collective-permute-start(f32[1,8,4,128]{3,2,1,0:T(4,128)S(1)} %pad_maximum_fusion.6), channel_id=1, source_target_pairs={{1,0},{2,1},{3,2},{4,3},{5,4},{6,5},{7,6},{9,8},{10,9},{11,10},{12... | collective-permute-start | bytes 49160 | tf_op jit(solution)/shard_map/while/body/eval_jaxpr/ppermute | solution.py:20
  87.8 6.6 %collective-permute-start.1 = (f32[1,8,4,128]{3,2,1,0:T(4,128)S(1)}, f32[1,8,4,128]{3,2,1,0:T(4,128)S(1)}, u32[]{:S(2)}, u32[]{:S(2)}) collective-permute-start(f32[1,8,4,128]{3,2,1,0:T(4,128)S(1)} %pad_maximum_fusion.6), channel_id=1, source_target_pairs={{0,1},{1,2},{2,3},{3,4},{4,5},{5,6},{6,7},{8,9},{9,10},{10,11},{11... | collective-permute-start | bytes 49160 | tf_op jit(solution)/shard_map/while/body/eval_jaxpr/ppermute | solution.py:17
  100.6 7.1 %collective-permute-start = (f32[1,8,4,128]{3,2,1,0:T(4,128)S(1)}, f32[1,8,4,128]{3,2,1,0:T(4,128)S(1)}, u32[]{:S(2)}, u32[]{:S(2)}) collective-permute-start(f32[1,8,4,128]{3,2,1,0:T(4,128)S(1)} %pad_maximum_fusion.6), channel_id=1, source_target_pairs={{1,0},{2,1},{3,2},{4,3},{5,4},{6,5},{7,6},{9,8},{10,9},{11,10},{12... | collective-permute-start | bytes 49160 | tf_op jit(solution)/shard_map/while/body/eval_jaxpr/ppermute | solution.py:20
  103.2 6.6 %collective-permute-start.1 = (f32[1,8,4,128]{3,2,1,0:T(4,128)S(1)}, f32[1,8,4,128]{3,2,1,0:T(4,128)S(1)}, u32[]{:S(2)}, u32[]{:S(2)}) collective-permute-start(f32[1,8,4,128]{3,2,1,0:T(4,128)S(1)} %pad_maximum_fusion.6), channel_id=1, source_target_pairs={{0,1},{1,2},{2,3},{3,4},{4,5},{5,6},{6,7},{8,9},{9,10},{10,11},{11... | collective-permute-start | bytes 49160 | tf_op jit(solution)/shard_map/while/body/eval_jaxpr/ppermute | solution.py:17
  116.0 7.1 %collective-permute-start = (f32[1,8,4,128]{3,2,1,0:T(4,128)S(1)}, f32[1,8,4,128]{3,2,1,0:T(4,128)S(1)}, u32[]{:S(2)}, u32[]{:S(2)}) collective-permute-start(f32[1,8,4,128]{3,2,1,0:T(4,128)S(1)} %pad_maximum_fusion.6), channel_id=1, source_target_pairs={{1,0},{2,1},{3,2},{4,3},{5,4},{6,5},{7,6},{9,8},{10,9},{11,10},{12... | collective-permute-start | bytes 49160 | tf_op jit(solution)/shard_map/while/body/eval_jaxpr/ppermute | solution.py:20
  118.6 6.6 %collective-permute-start.1 = (f32[1,8,4,128]{3,2,1,0:T(4,128)S(1)}, f32[1,8,4,128]{3,2,1,0:T(4,128)S(1)}, u32[]{:S(2)}, u32[]{:S(2)}) collective-permute-start(f32[1,8,4,128]{3,2,1,0:T(4,128)S(1)} %pad_maximum_fusion.6), channel_id=1, source_target_pairs={{0,1},{1,2},{2,3},{3,4},{4,5},{5,6},{6,7},{8,9},{9,10},{10,11},{11... | collective-permute-start | bytes 49160 | tf_op jit(solution)/shard_map/while/body/eval_jaxpr/ppermute | solution.py:17
  131.4 7.1 %collective-permute-start = (f32[1,8,4,128]{3,2,1,0:T(4,128)S(1)}, f32[1,8,4,128]{3,2,1,0:T(4,128)S(1)}, u32[]{:S(2)}, u32[]{:S(2)}) collective-permute-start(f32[1,8,4,128]{3,2,1,0:T(4,128)S(1)} %pad_maximum_fusion.6), channel_id=1, source_target_pairs={{1,0},{2,1},{3,2},{4,3},{5,4},{6,5},{7,6},{9,8},{10,9},{11,10},{12... | collective-permute-start | bytes 49160 | tf_op jit(solution)/shard_map/while/body/eval_jaxpr/ppermute | solution.py:20
  134.0 6.6 %collective-permute-start.1 = (f32[1,8,4,128]{3,2,1,0:T(4,128)S(1)}, f32[1,8,4,128]{3,2,1,0:T(4,128)S(1)}, u32[]{:S(2)}, u32[]{:S(2)}) collective-permute-start(f32[1,8,4,128]{3,2,1,0:T(4,128)S(1)} %pad_maximum_fusion.6), channel_id=1, source_target_pairs={{0,1},{1,2},{2,3},{3,4},{4,5},{5,6},{6,7},{8,9},{9,10},{10,11},{11... | collective-permute-start | bytes 49160 | tf_op jit(solution)/shard_map/while/body/eval_jaxpr/ppermute | solution.py:17
  146.8 7.1 %collective-permute-start = (f32[1,8,4,128]{3,2,1,0:T(4,128)S(1)}, f32[1,8,4,128]{3,2,1,0:T(4,128)S(1)}, u32[]{:S(2)}, u32[]{:S(2)}) collective-permute-start(f32[1,8,4,128]{3,2,1,0:T(4,128)S(1)} %pad_maximum_fusion.6), channel_id=1, source_target_pairs={{1,0},{2,1},{3,2},{4,3},{5,4},{6,5},{7,6},{9,8},{10,9},{11,10},{12... | collective-permute-start | bytes 49160 | tf_op jit(solution)/shard_map/while/body/eval_jaxpr/ppermute | solution.py:20
  149.4 6.6 %collective-permute-start.1 = (f32[1,8,4,128]{3,2,1,0:T(4,128)S(1)}, f32[1,8,4,128]{3,2,1,0:T(4,128)S(1)}, u32[]{:S(2)}, u32[]{:S(2)}) collective-permute-start(f32[1,8,4,128]{3,2,1,0:T(4,128)S(1)} %pad_maximum_fusion.6), channel_id=1, source_target_pairs={{0,1},{1,2},{2,3},{3,4},{4,5},{5,6},{6,7},{8,9},{9,10},{10,11},{11... | collective-permute-start | bytes 49160 | tf_op jit(solution)/shard_map/while/body/eval_jaxpr/ppermute | solution.py:17
  162.2 7.1 %collective-permute-start = (f32[1,8,4,128]{3,2,1,0:T(4,128)S(1)}, f32[1,8,4,128]{3,2,1,0:T(4,128)S(1)}, u32[]{:S(2)}, u32[]{:S(2)}) collective-permute-start(f32[1,8,4,128]{3,2,1,0:T(4,128)S(1)} %pad_maximum_fusion.6), channel_id=1, source_target_pairs={{1,0},{2,1},{3,2},{4,3},{5,4},{6,5},{7,6},{9,8},{10,9},{11,10},{12... | collective-permute-start | bytes 49160 | tf_op jit(solution)/shard_map/while/body/eval_jaxpr/ppermute | solution.py:20
  164.8 6.6 %collective-permute-start.1 = (f32[1,8,4,128]{3,2,1,0:T(4,128)S(1)}, f32[1,8,4,128]{3,2,1,0:T(4,128)S(1)}, u32[]{:S(2)}, u32[]{:S(2)}) collective-permute-start(f32[1,8,4,128]{3,2,1,0:T(4,128)S(1)} %pad_maximum_fusion.6), channel_id=1, source_target_pairs={{0,1},{1,2},{2,3},{3,4},{4,5},{5,6},{6,7},{8,9},{9,10},{10,11},{11... | collective-permute-start | bytes 49160 | tf_op jit(solution)/shard_map/while/body/eval_jaxpr/ppermute | solution.py:17
  177.6 7.1 %collective-permute-start = (f32[1,8,4,128]{3,2,1,0:T(4,128)S(1)}, f32[1,8,4,128]{3,2,1,0:T(4,128)S(1)}, u32[]{:S(2)}, u32[]{:S(2)}) collective-permute-start(f32[1,8,4,128]{3,2,1,0:T(4,128)S(1)} %pad_maximum_fusion.6), channel_id=1, source_target_pairs={{1,0},{2,1},{3,2},{4,3},{5,4},{6,5},{7,6},{9,8},{10,9},{11,10},{12... | collective-permute-start | bytes 49160 | tf_op jit(solution)/shard_map/while/body/eval_jaxpr/ppermute | solution.py:20
  180.2 6.6 %collective-permute-start.1 = (f32[1,8,4,128]{3,2,1,0:T(4,128)S(1)}, f32[1,8,4,128]{3,2,1,0:T(4,128)S(1)}, u32[]{:S(2)}, u32[]{:S(2)}) collective-permute-start(f32[1,8,4,128]{3,2,1,0:T(4,128)S(1)} %pad_maximum_fusion.6), channel_id=1, source_target_pairs={{0,1},{1,2},{2,3},{3,4},{4,5},{5,6},{6,7},{8,9},{9,10},{10,11},{11... | collective-permute-start | bytes 49160 | tf_op jit(solution)/shard_map/while/body/eval_jaxpr/ppermute | solution.py:17
  193.0 7.1 %collective-permute-start = (f32[1,8,4,128]{3,2,1,0:T(4,128)S(1)}, f32[1,8,4,128]{3,2,1,0:T(4,128)S(1)}, u32[]{:S(2)}, u32[]{:S(2)}) collective-permute-start(f32[1,8,4,128]{3,2,1,0:T(4,128)S(1)} %pad_maximum_fusion.6), channel_id=1, source_target_pairs={{1,0},{2,1},{3,2},{4,3},{5,4},{6,5},{7,6},{9,8},{10,9},{11,10},{12... | collective-permute-start | bytes 49160 | tf_op jit(solution)/shard_map/while/body/eval_jaxpr/ppermute | solution.py:20
  195.6 6.6 %collective-permute-start.1 = (f32[1,8,4,128]{3,2,1,0:T(4,128)S(1)}, f32[1,8,4,128]{3,2,1,0:T(4,128)S(1)}, u32[]{:S(2)}, u32[]{:S(2)}) collective-permute-start(f32[1,8,4,128]{3,2,1,0:T(4,128)S(1)} %pad_maximum_fusion.6), channel_id=1, source_target_pairs={{0,1},{1,2},{2,3},{3,4},{4,5},{5,6},{6,7},{8,9},{9,10},{10,11},{11... | collective-permute-start | bytes 49160 | tf_op jit(solution)/shard_map/while/body/eval_jaxpr/ppermute | solution.py:17
  208.1 64.8 %copy-start = (f32[8,128,128]{2,1,0:T(8,128)S(1)}, f32[8,128,128]{2,1,0:T(8,128)}, u32[]{:S(2)}) copy-start(f32[8,128,128]{2,1,0:T(8,128)} %param.19) | copy-start | bytes 1572868
  324.3 12.1 %copy-start.2 = (f32[1,8,128,128]{3,2,1,0:T(8,128)S(1)}, f32[1,8,128,128]{3,2,1,0:T(8,128)}, u32[]{:S(2)}) copy-start(f32[1,8,128,128]{3,2,1,0:T(8,128)} %param.12) | copy-start | bytes 1572868
  327.1 10.2 %copy-start.4 = (f32[1,8,128,128]{3,2,1,0:T(8,128)}, f32[1,8,128,128]{3,2,1,0:T(8,128)S(1)}, u32[]{:S(2)}) copy-start(f32[1,8,128,128]{3,2,1,0:T(8,128)S(1)} %add.163) | copy-start | bytes 1572868
  327.1 9.3 %collective-permute-start.2 = (f32[8,128,128]{2,1,0:T(8,128)S(1)}, f32[8,128,128]{2,1,0:T(8,128)S(1)}, u32[]{:S(2)}, u32[]{:S(2)}) collective-permute-start(f32[8,128,128]{2,1,0:T(8,128)S(1)} %bitcast.111), channel_id=1, source_target_pairs={{0,8},{8,16},{16,24},{24,32},{32,40},{40,48},{48,56},{56,64},{64,7... | collective-permute-start | bytes 1572872 | tf_op jit(solution)/shard_map/ppermute | solution.py:32
  (3 other events, 25.1 us)
Sparse Core Ops, SparseCore 0:
  10.5 55.1 all-gather.5
  213.4 59.5 all-gather.3
where the time goes:
time: 351 us; the launch traced here: 344 us
  waiting for transfers between devices  91 us (26%)
  local copies, waits for them, and re-layouts  82.9 us (24%)
  starting transfers between devices  69 us (20%)
  matrix products  45.3 us (13%)
  other arithmetic  40.1 us (11%)
  between operations  14.3 us (4%)
    all_gather x1, waiting for transfers between devices, on_device(): every_jump = lax.all_gather(coarse_jump, 'tm', axis=0, tiled=True)  58.7 us
    dot_general x18, matrix products, apply_coarse(): jnp.einsum('...tik,tlk->...til', mixed_x, matrix_y, precision=exact_preci...  36.4 us
    mul x12, other arithmetic, advance(): open_cells * (current + strength * diffusivity * laplace - 0.5 * transport)  35.3 us
    ppermute x12, starting transfers between devices, padded(): lax.ppermute(lax.slice_in_dim(block, 0, width, axis=dim), axis, backward)  33.9 us
    ppermute x12, starting transfers between devices, padded(): lax.ppermute(lax.slice_in_dim(block, block.shape[dim] - width, None, axis...  31.8 us
    ppermute x12, waiting for transfers between devices, padded(): lax.ppermute(lax.slice_in_dim(block, block.shape[dim] - width, None, axis...  26.1 us
    dynamic_update_slice x16, local copies, waits for them, and re-layouts, on_device(): last_state, history = lax.scan(sweep, first_coarse, every_jump)  11.7 us
    slice x12, local copies, waits for them, and re-layouts, advance(): current[:, :, :, :-1]  10.5 us
  transfers between devices with their start and end apart: 27, of which 14 were waited for; matrix products, arithmetic and copies ran while one was open for 32% of the time, Pallas kernels for 0%

commit v1 on v0

v1 whole, which is shorter than its diff:
```python
import jax
import jax.numpy as jnp
from jax import lax
from jax.experimental import pallas as pl
from jax.experimental.pallas import tpu as pltpu
from jax.sharding import PartitionSpec as P

MESH = pl.DeviceIdType.MESH
SUB = 12
PLACES = 8
TILE = 128
CX = 64
SLICES = 16
BLOCK = 32
F32 = jnp.float32
BF16 = jnp.bfloat16


def halves(value):
    high = value.astype(BF16)
    return high, (value - high.astype(F32)).astype(BF16)


def product(left, right):
    left_high, left_low = left
    right_high, right_low = right
    total = jnp.dot(left_high, right_low, preferred_element_type=F32)
    total = total + jnp.dot(left_low, right_high, preferred_element_type=F32)
    return total + jnp.dot(left_high, right_high, preferred_element_type=F32)


def place_order(neighbors, space):
    first = jnp.int32(0)
    for t in range(PLACES):
        first = first + jnp.where(neighbors[t, 2] == PLACES * 8, t, 0)
    first = jnp.clip(first, 0, PLACES - 1)
    order = [first]
    for _ in range(PLACES - 1):
        order.append(jnp.clip(neighbors[order[-1], 3] - space * PLACES, 0, PLACES - 1))
    return order


def fine_kernel(
    scale, neighbors, starts_hbm, diff_hbm, vel_hbm, obst_hbm, cx_hbm, cy_hbm,
    sum_out, coarse_out, half_out, prev_out,
    starts, diff, vel, obst, cx, cy, load_sem,
    state, coef_d, coef_a, coef_b, west, east, west_past, east_past,
    xh, xl, yh, yl, coarse_starts, coarse_ends, mean, jump, half, half_prev,
    jumps, chain, coarse,
    halo_ss, halo_rs, jump_ss, jump_rs, half_ss, half_rs, chain_ss, chain_rs,
):
    tm = lax.axis_index("tm")
    space = lax.axis_index("space")
    core = lax.rem(tm, 2)
    chip = tm // 2
    is_owner = core == 0

    loads = [
        pltpu.make_async_copy(src, dst, load_sem.at[i])
        for i, (src, dst) in enumerate(
            [(starts_hbm, starts), (diff_hbm, diff), (obst_hbm, obst), (vel_hbm, vel),
             (cx_hbm, cx), (cy_hbm, cy)]
        )
    ]
    for load in loads:
        load.start()

    barrier = pltpu.get_barrier_semaphore()

    def greet(target_tm, target_space):
        pl.semaphore_signal(
            barrier, inc=1, device_id=(target_tm, target_space), device_id_type=MESH
        )

    @pl.when(space > 0)
    def _():
        greet(tm, space - 1)

    @pl.when(space < 7)
    def _():
        greet(tm, space + 1)

    def greet_slice(i, carry):
        greet(lax.rem(tm + i, SLICES), space)
        return carry

    lax.fori_loop(1, SLICES, greet_slice, 0)

    order = place_order(neighbors, space)

    for load in loads[:4]:
        load.wait()
    for p in range(PLACES):
        t = order[p]

        def convert(i, carry):
            rows = pl.ds(pl.multiple_of(i * 8, 8), 8)
            spread = pl.ds(i * 64 + p, 8, stride=8)
            open_cells = 1.0 - obst[t, rows, :].astype(F32)
            state[spread, :] = starts[t, rows, :]
            coef_d[spread, :] = open_cells * diff[t, rows, :]
            coef_a[spread, :] = (0.5 * open_cells) * vel[0, t, rows, :]
            coef_b[spread, :] = (0.5 * open_cells) * vel[1, t, rows, :]
            return carry

        lax.fori_loop(0, TILE // 8, convert, 0, unroll=4)

    def row(ref, r):
        at = r * 8 if isinstance(r, int) else pl.multiple_of(r * 8, 8)
        return ref[pl.ds(at, 8), :]

    state[pl.ds(TILE * 8, 8), :] = jnp.zeros((8, TILE), F32)
    for q, ref in enumerate((state, coef_d, coef_a, coef_b)):
        for i in range(SUB):
            west[q, SUB + i] = row(ref, i)
            east[q, i] = row(ref, TILE - SUB + i)

    @pl.when(space == 0)
    def _():
        west[:, 0:SUB] = jnp.zeros((4, SUB, 8, TILE), F32)

    @pl.when(space == 7)
    def _():
        east[:, SUB : 2 * SUB] = jnp.zeros((4, SUB, 8, TILE), F32)

    greeted = SLICES - 1 + jnp.where(space > 0, 1, 0) + jnp.where(space < 7, 1, 0)
    pl.semaphore_wait(barrier, greeted)

    to_west = pltpu.make_async_remote_copy(
        west.at[:, SUB : 2 * SUB], east.at[:, SUB : 2 * SUB], halo_ss.at[0], halo_rs.at[1],
        device_id=(tm, jnp.maximum(space - 1, 0)), device_id_type=MESH,
    )
    to_east = pltpu.make_async_remote_copy(
        east.at[:, 0:SUB], west.at[:, 0:SUB], halo_ss.at[1], halo_rs.at[0],
        device_id=(tm, jnp.minimum(space + 1, 7)), device_id_type=MESH,
    )

    @pl.when(space > 0)
    def _():
        to_west.start()

    @pl.when(space < 7)
    def _():
        to_east.start()

    lane = lax.broadcasted_iota(jnp.int32, (8, TILE), 1)
    sub = lax.broadcasted_iota(jnp.int32, (8, TILE), 0)
    south_face = lane == 0
    north_face = lane == TILE - 1
    south_end = jnp.logical_and(south_face, sub == 0)
    north_end = jnp.logical_and(north_face, sub == 7)

    def update(before, now, after, d, a, b, strength):
        south = pltpu.roll(now, 1, 1)
        south = jnp.where(south_face, pltpu.roll(south, 1, 0), south)
        south = jnp.where(south_end, 0.0, south)
        north = pltpu.roll(now, TILE - 1, 1)
        north = jnp.where(north_face, pltpu.roll(north, 7, 0), north)
        north = jnp.where(north_end, 0.0, north)
        laplace = (before + after) + (south + north) - 4.0 * now
        kept = jnp.where(d > 0.0, now, 0.0)
        return (
            kept + (strength * d) * laplace - a * (after - before) - b * (north - south)
        )

    for load in loads[4:]:
        load.wait()
    for p in range(PLACES):
        t = order[p]
        x_high, x_low = halves(cx[t])
        xh[p] = x_high
        xl[p] = x_low
        y_high, y_low = halves(cy[t].T)
        yh[p] = y_high
        yl[p] = y_low
        coarse_starts[p] = 0.5 * (
            starts[t, pl.ds(0, CX, stride=2), :] + starts[t, pl.ds(1, CX, stride=2), :]
        )

    def apply_coarse(p, values):
        mixed = product((xh[p], xl[p]), halves(values))
        return product(halves(mixed), (yh[p], yl[p]))

    for p in range(PLACES):
        coarse_ends[pl.ds(p * CX, CX), :] = apply_coarse(p, coarse_starts[p])

    def substep(s, carry):
        strength = scale[s]
        west_past[s, 0] = row(state, s)
        west_past[s, 1] = row(state, s + 1)
        east_past[s, 0] = row(state, TILE - 1 - s)
        east_past[s, 1] = row(state, TILE - 2 - s)

        def rows(i, before):
            base = i * BLOCK
            now = row(state, base)
            for r in range(BLOCK):
                at = base + r
                after = row(state, at + 1)
                fresh = update(
                    before, now, after, row(coef_d, at), row(coef_a, at), row(coef_b, at), strength
                )
                state[pl.ds(pl.multiple_of(at * 8, 8), 8), :] = fresh
                before, now = now, after
            return before

        lax.fori_loop(0, TILE // BLOCK, rows, jnp.zeros((8, TILE), F32))
        return carry

    lax.fori_loop(0, SUB, substep, 0)

    first_slice = jnp.where(tm == 0, 1.0, 0.0)

    def settle(i, even, odd):
        spread = pl.ds(i, 8, stride=CX)
        middle = 0.5 * (even + odd)
        coarse_end = coarse_ends[spread, :]
        mean[spread, :] = middle - coarse_end
        jump[spread, :] = middle - coarse_end + first_slice * coarse_end
        half[spread, :] = 0.5 * (even - odd)

    def settle_inner(i, carry):
        settle(i, row(state, 2 * i), row(state, 2 * i + 1))
        return carry

    lax.fori_loop(SUB // 2, CX - SUB // 2, settle_inner, 0, unroll=4)

    @pl.when(space > 0)
    def _():
        to_west.wait_send()
        to_east.wait_recv()

    @pl.when(space < 7)
    def _():
        to_east.wait_send()
        to_west.wait_recv()

    def border(s, carry):
        strength = scale[s]
        before = west[0, s]
        now = west[0, s + 1]
        for w in range(SUB):
            at = s + 1 + w
            after = west[0, at + 1] if w < SUB - 2 else west_past[s, w - (SUB - 2)]
            west[0, at] = update(
                before, now, after, west[1, at], west[2, at], west[3, at], strength
            )
            before, now = now, after
        after = east[0, 2 * SUB - 1 - s]
        now = east[0, 2 * SUB - 2 - s]
        for w in range(SUB):
            at = 2 * SUB - 2 - s - w
            before = east[0, at - 1] if w < SUB - 2 else east_past[s, w - (SUB - 2)]
            east[0, at] = update(
                before, now, after, east[1, at], east[2, at], east[3, at], strength
            )
            after, now = now, before
        return carry

    lax.fori_loop(0, SUB, border, 0)
    for i in range(SUB // 2):
        settle(i, west[0, SUB + 2 * i], west[0, SUB + 2 * i + 1])
        settle(CX - SUB // 2 + i, east[0, 2 * i], east[0, 2 * i + 1])

    def jump_copy(p):
        return pltpu.make_async_remote_copy(
            jump.at[pl.ds(p * CX, CX), :], jumps.at[tm], jump_ss.at[p], jump_rs.at[tm],
            device_id=(2 * p, space), device_id_type=MESH,
        )

    def jump_arrival(n):
        return pltpu.make_async_remote_copy(
            jump.at[pl.ds(0, CX), :], jumps.at[n], jump_ss.at[0], jump_rs.at[n],
            device_id=(tm, space), device_id_type=MESH,
        )

    for p in range(PLACES):
        @pl.when(jnp.logical_and(tm != 2 * p, tm < SLICES - 1))
        def _(p=p):
            jump_copy(p).start()

    half_copy = pltpu.make_async_remote_copy(
        half, half_prev, half_ss, half_rs,
        device_id=(jnp.minimum(tm + 1, SLICES - 1), space), device_id_type=MESH,
    )

    @pl.when(tm < SLICES - 1)
    def _():
        half_copy.start()

    def state_copy(n):
        return pltpu.make_async_remote_copy(
            chain.at[n], coarse.at[chip], chain_ss.at[n], chain_rs.at[chip],
            device_id=(n, space), device_id_type=MESH,
        )

    def state_arrival(p):
        return pltpu.make_async_remote_copy(
            chain.at[0], coarse.at[p], chain_ss.at[0], chain_rs.at[p],
            device_id=(tm, space), device_id_type=MESH,
        )

    @pl.when(is_owner)
    def _():
        jumps[tm] = jump[pl.ds(pl.multiple_of(chip * CX, CX), CX), :]

        def link(n, values):
            @pl.when(n != tm)
            def _():
                jump_arrival(n).wait_recv()

            values = jumps[n] + jnp.where(n > 0, 1.0, 0.0) * apply_coarse(chip, values)
            chain[n + 1] = values

            @pl.when(n + 1 != tm)
            def _():
                state_copy(n + 1).start()

            @pl.when(n + 1 == tm)
            def _():
                coarse[chip] = values

            return values

        lax.fori_loop(0, SLICES - 1, link, jnp.zeros((CX, TILE), F32))

    @pl.when(tm == 0)
    def _():
        coarse[...] = coarse_starts[...]

    half_out[...] = half[...]

    for p in range(PLACES):
        remote = jnp.logical_and(tm > 0, tm != 2 * p)

        @pl.when(remote)
        def _(p=p):
            state_arrival(p).wait_recv()

        values = coarse[p]
        coarse_out[pl.ds(p * CX, CX), :] = values
        sum_out[pl.ds(p * CX, CX), :] = apply_coarse(p, values) + mean[pl.ds(p * CX, CX), :]

    @pl.when(tm > 0)
    def _():
        half_copy.wait_recv()
        prev_out[...] = half_prev[...]

    @pl.when(tm == 0)
    def _():
        prev_out[...] = jnp.zeros_like(prev_out)

    for p in range(PLACES):
        @pl.when(jnp.logical_and(tm != 2 * p, tm < SLICES - 1))
        def _(p=p):
            jump_copy(p).wait_send()

    @pl.when(tm < SLICES - 1)
    def _():
        half_copy.wait_send()

    @pl.when(is_owner)
    def _():
        def sent(n, carry):
            @pl.when(n != tm)
            def _():
                state_copy(n).wait_send()

            return carry

        lax.fori_loop(1, SLICES, sent, 0)


def finish_kernel(neighbors, starts, sums, coarse, half, prev, ends_out, step_out):
    tm = lax.axis_index("tm")
    order = place_order(neighbors, lax.axis_index("space"))
    later = jnp.where(tm > 0, 1.0, 0.0)
    for p in range(PLACES):
        t = order[p]
        rows = pl.ds(p * CX, CX)
        even, odd = pl.ds(0, CX, stride=2), pl.ds(1, CX, stride=2)
        total, difference = sums[rows, :], half[rows, :]
        ends_out[t, even, :] = total + difference
        ends_out[t, odd, :] = total - difference
        total, difference = coarse[rows, :], prev[rows, :]
        step_out[t, even, :] = later * (total + difference - starts[t, even, :])
        step_out[t, odd, :] = later * (total - difference - starts[t, odd, :])


def on_device(
    starts, diffusivity, velocity, obstacle, substep_scale, neighbors, coarse_x, coarse_y
):
    smem = pl.BlockSpec(memory_space=pltpu.SMEM)
    vmem = pl.BlockSpec(memory_space=pltpu.VMEM)
    anywhere = pl.BlockSpec(memory_space=pl.ANY)
    tiles = (PLACES, TILE, TILE)
    places = jax.ShapeDtypeStruct((PLACES * CX, TILE), F32)
    dma = pltpu.SemaphoreType.DMA
    starts = starts[0]
    sums, coarse, half, prev = pl.pallas_call(
        fine_kernel,
        out_shape=(places,) * 4,
        in_specs=[smem, smem] + [anywhere] * 6,
        out_specs=(vmem,) * 4,
        scratch_shapes=[
            pltpu.VMEM(tiles, F32),
            pltpu.VMEM(tiles, F32),
            pltpu.VMEM((2,) + tiles, F32),
            pltpu.VMEM(tiles, jnp.int32),
            pltpu.VMEM((PLACES, CX, CX), F32),
            pltpu.VMEM(tiles, F32),
            dma((6,)),
            pltpu.VMEM((TILE * 8 + 8, TILE), F32),
            pltpu.VMEM((TILE * 8, TILE), F32),
            pltpu.VMEM((TILE * 8, TILE), F32),
            pltpu.VMEM((TILE * 8, TILE), F32),
            pltpu.VMEM((4, 2 * SUB, 8, TILE), F32),
            pltpu.VMEM((4, 2 * SUB, 8, TILE), F32),
            pltpu.VMEM((SUB, 2, 8, TILE), F32),
            pltpu.VMEM((SUB, 2, 8, TILE), F32),
            pltpu.VMEM((PLACES, CX, CX), BF16),
            pltpu.VMEM((PLACES, CX, CX), BF16),
            pltpu.VMEM(tiles, BF16),
            pltpu.VMEM(tiles, BF16),
            pltpu.VMEM((PLACES, CX, TILE), F32),
            pltpu.VMEM((PLACES * CX, TILE), F32),
            pltpu.VMEM((PLACES * CX, TILE), F32),
            pltpu.VMEM((PLACES * CX, TILE), F32),
            pltpu.VMEM((PLACES * CX, TILE), F32),
            pltpu.VMEM((PLACES * CX, TILE), F32),
            pltpu.VMEM((SLICES, CX, TILE), F32),
            pltpu.VMEM((SLICES, CX, TILE), F32),
            pltpu.VMEM((PLACES, CX, TILE), F32),
            dma((2,)),
            dma((2,)),
            dma((PLACES,)),
            dma((SLICES,)),
            dma,
            dma,
            dma((SLICES,)),
            dma((PLACES,)),
        ],
        compiler_params=pltpu.CompilerParams(
            collective_id=0, has_side_effects=True, vmem_limit_bytes=60 << 20
        ),
    )(substep_scale, neighbors, starts, diffusivity, velocity, obstacle, coarse_x, coarse_y)
    ends, step = pl.pallas_call(
        finish_kernel,
        out_shape=(jax.ShapeDtypeStruct(tiles, F32),) * 2,
        in_specs=[smem] + [vmem] * 5,
        out_specs=(vmem, vmem),
        compiler_params=pltpu.CompilerParams(vmem_limit_bytes=40 << 20),
    )(neighbors, starts, sums, coarse, half, prev)
    return ends[None], step[None]


def solution(mesh):
    placed = (
        P("tm", "space", None, None),
        P("space", None, None),
        P(None, "space", None, None),
        P("space", None, None),
        P(),
        P("space", None),
        P("space", None, None),
        P("space", None, None),
    )
    return jax.shard_map(
        on_device,
        mesh=mesh,
        in_specs=placed,
        out_specs=(P("tm", "space", None, None), P("tm", "space", None, None)),
        check_vma=False,
    )
```

time: 351 us -> 46.3 us (0.13); the launches traced: 344 us -> 45.9 us
  waiting for transfers between devices: 91 us -> 0 us
  local copies, waits for them, and re-layouts: 82.9 us -> 5.82 us
  starting transfers between devices: 69 us -> 0 us
  matrix products: 45.3 us -> 0 us
  other arithmetic: 40.1 us -> 0 us
  Pallas kernels: 0 us -> 39.4 us
  between operations: 14.3 us -> 0.66 us
    ppermute x25 -> x0, starting transfers between devices: 68.9 us -> none  [the longest x12 33.9 us: padded(): lax.ppermute(lax.slice_in_dim(block, 0, width, axis=dim), axis, backward)]
    all_gather x2 -> x0, waiting for transfers between devices: 58.7 us -> none  [the longest x1 58.7 us: on_device(): every_jump = lax.all_gather(coarse_jump, 'tm', axis=0, tiled=True)]
    dot_general x36 -> x0, matrix products: 45.3 us -> none  [the longest x18 36.4 us: apply_coarse(): jnp.einsum('...tik,tlk->...til', mixed_x, matrix_y, precision=exact_preci...]
    pallas_call x0 -> x2, Pallas kernels: none -> 39.4 us  [the longest x1 37.7 us: on_device(): pl.pallas_call(fine_kernel, out_shape=(places,) * 4, in_specs=[smem, smem...]
    mul x14 -> x0, other arithmetic: 36.8 us -> none  [the longest x12 35.3 us: advance(): open_cells * (current + strength * diffusivity * laplace - 0.5 * transport)]
    ppermute x25 -> x0, waiting for transfers between devices: 32.3 us -> none  [the longest x12 26.1 us: padded(): lax.ppermute(lax.slice_in_dim(block, block.shape[dim] - width, None, axis...]
    gather x48 -> x0, local copies, waits for them, and re-layouts: 28 us -> none  [the longest x12 7 us: advance(): north_face = gathered[:, lookup_index[:, 3], 2]]
    slice x55 -> x0, local copies, waits for them, and re-layouts: 18.9 us -> none  [the longest x12 10.5 us: advance(): current[:, :, :, :-1]]
  transfers between devices with their start and end apart: 27 -> 0, of which waited for: 14 -> 0; matrix products, arithmetic and copies ran while one was open for 32% -> 0% of each run, Pallas kernels for 0% -> 0%
where the time goes in v1:
time: 46.3 us; the launch traced here: 45.9 us
  Pallas kernels  39.4 us (85%)
  local copies, waits for them, and re-layouts  5.82 us (13%)
  between operations  0.66 us (1%)
    pallas_call x1, Pallas kernels, on_device(): pl.pallas_call(fine_kernel, out_shape=(places,) * 4, in_specs=[smem, smem...  37.7 us
    unnamed x13, local copies, waits for them, and re-layouts  5.82 us
    pallas_call x1, Pallas kernels, on_device(): pl.pallas_call(finish_kernel, out_shape=(jax.ShapeDtypeStruct(tiles, F32)...  1.71 us

profile of v1, /device:TPU:27, one launch (start us, length us, event | category | flops | bytes accessed | tf_op | source)
XLA Modules:
  0.0 45.9 jit_solution(15184437572766543270)
XLA Ops:
  0.6 1.3 %copy.11.neighbors = s32[8,4]{1,0:T(8,128)} copy(s32[8,4]{0,1:T(4,128)} %param.13) | data formatting | bytes 256 | tf_op args[5]
  2.0 0.0 copy-start
  2.0 37.7 %shard_map.95 = (f32[512,128]{1,0:T(8,128)}, f32[512,128]{1,0:T(8,128)}, f32[512,128]{1,0:T(8,128)}, f32[512,128]{1,0:T(8,128)}) custom-call(f32[12]{0:T(128)} %scale.1, s32[8,4]{1,0:T(8,128)} %copy.11.neighbors, f32[8,128,128]{2,1,0:T(8,128)} %bitcast.3, f32[8,128,128]{2,1,0:T(8,128)} %diff_hbm.1, f32[2,8,128,128]{3,2,1,0:T(8,128)} %vel_hbm.1, ...), custom_call_target="tpu_custom_call" | custom-call | tf_op jit(solution)/shard_map/pallas_call | solution.py:400
  39.7 0.0 copy-start.5
  39.7 0.0 copy-done
  39.8 0.7 %copy-done.5 = s32[8,4]{1,0:T(8,128)S(1)} copy-done((s32[8,4]{1,0:T(8,128)S(1)}, s32[8,4]{1,0:T(8,128)}, u32[]{:S(2)}) %copy-start.5) | copy-done | bytes 152
  40.4 0.0 copy-start.1
  40.4 0.9 %copy-done.1 = f32[512,128]{1,0:T(8,128)S(1)} copy-done((f32[512,128]{1,0:T(8,128)S(1)}, f32[512,128]{1,0:T(8,128)}, u32[]{:S(2)}) %copy-start.1) | copy-done | bytes 262168
  41.4 0.0 copy-start.2
  41.4 0.9 %copy-done.2 = f32[512,128]{1,0:T(8,128)S(1)} copy-done((f32[512,128]{1,0:T(8,128)S(1)}, f32[512,128]{1,0:T(8,128)}, u32[]{:S(2)}) %copy-start.2) | copy-done | bytes 262168
  42.3 0.0 copy-start.3
  42.3 0.9 %copy-done.3 = f32[512,128]{1,0:T(8,128)S(1)} copy-done((f32[512,128]{1,0:T(8,128)S(1)}, f32[512,128]{1,0:T(8,128)}, u32[]{:S(2)}) %copy-start.3) | copy-done | bytes 262168
  43.3 0.0 copy-start.4
  43.3 0.9 %copy-done.4 = f32[512,128]{1,0:T(8,128)S(1)} copy-done((f32[512,128]{1,0:T(8,128)S(1)}, f32[512,128]{1,0:T(8,128)}, u32[]{:S(2)}) %copy-start.4) | copy-done | bytes 262168
  44.2 1.7 %shard_map.96 = (f32[8,128,128]{2,1,0:T(8,128)}, f32[8,128,128]{2,1,0:T(8,128)}) custom-call(s32[8,4]{1,0:T(8,128)S(1)} %copy-done.5, f32[8,128,128]{2,1,0:T(8,128)S(1)} %bitcast.4, f32[512,128]{1,0:T(8,128)S(1)} %copy-done.1, f32[512,128]{1,0:T(8,128)S(1)} %copy-done.2, f32[512,128]{1,0:T(8,128)S(1)} %copy-done.3, f32[512,128]{1,0:T(8,128)S(1)} %copy-done.4), custom_call_target="tpu_custom_call" | custom-call | tf_op jit(solution)/shard_map/pallas_call | solution.py:447
Async XLA Ops:
  2.0 37.8 %copy-start = (f32[1,8,128,128]{3,2,1,0:T(8,128)S(1)}, f32[1,8,128,128]{3,2,1,0:T(8,128)}, u32[]{:S(2)}) copy-start(f32[1,8,128,128]{3,2,1,0:T(8,128)} %param.8) | copy-start | bytes 1572868
  39.7 0.7 %copy-start.5 = (s32[8,4]{1,0:T(8,128)S(1)}, s32[8,4]{1,0:T(8,128)}, u32[]{:S(2)}) copy-start(s32[8,4]{1,0:T(8,128)} %copy.11.neighbors) | copy-start | bytes 388
  40.4 0.9 %copy-start.1 = (f32[512,128]{1,0:T(8,128)S(1)}, f32[512,128]{1,0:T(8,128)}, u32[]{:S(2)}) copy-start(f32[512,128]{1,0:T(8,128)} %get-tuple-element.8.sums) | copy-start | bytes 786436
  41.4 0.9 %copy-start.2 = (f32[512,128]{1,0:T(8,128)S(1)}, f32[512,128]{1,0:T(8,128)}, u32[]{:S(2)}) copy-start(f32[512,128]{1,0:T(8,128)} %get-tuple-element.9.coarse) | copy-start | bytes 786436
  42.3 0.9 %copy-start.3 = (f32[512,128]{1,0:T(8,128)S(1)}, f32[512,128]{1,0:T(8,128)}, u32[]{:S(2)}) copy-start(f32[512,128]{1,0:T(8,128)} %get-tuple-element.10.half) | copy-start | bytes 786436
  43.3 0.9 %copy-start.4 = (f32[512,128]{1,0:T(8,128)S(1)}, f32[512,128]{1,0:T(8,128)}, u32[]{:S(2)}) copy-start(f32[512,128]{1,0:T(8,128)} %get-tuple-element.11.prev) | copy-start | bytes 786436

commit v2 on v1

--- a/solution.py
+++ b/solution.py
@@ -10,6 +10,7 @@
 PLACES = 8
 TILE = 128
 CX = 64
+MID = 48
 SLICES = 16
 BLOCK = 32
 F32 = jnp.float32
@@ -32,11 +33,11 @@
 def place_order(neighbors, space):
     first = jnp.int32(0)
     for t in range(PLACES):
-        first = first + jnp.where(neighbors[t, 2] == PLACES * 8, t, 0)
+        first = first + jnp.where(neighbors[2, t] == PLACES * 8, t, 0)
     first = jnp.clip(first, 0, PLACES - 1)
     order = [first]
     for _ in range(PLACES - 1):
-        order.append(jnp.clip(neighbors[order[-1], 3] - space * PLACES, 0, PLACES - 1))
+        order.append(jnp.clip(neighbors[3, order[-1]] - space * PLACES, 0, PLACES - 1))
     return order
 
 
@@ -45,8 +46,9 @@
     sum_out, coarse_out, half_out, prev_out,
     starts, diff, vel, obst, cx, cy, load_sem,
     state, coef_d, coef_a, coef_b, west, east, west_past, east_past,
-    xh, xl, yh, yl, coarse_starts, coarse_ends, mean, jump, half, half_prev,
-    jumps, chain, coarse,
+    xh, xl, yh, yl, coarse_starts, coarse_ends, mean, half,
+    jump_mid, jump_edge, half_mid, half_edge, prev_mid, prev_edge, jumps_mid, jumps_edge,
+    chain, coarse,
     halo_ss, halo_rs, jump_ss, jump_rs, half_ss, half_rs, chain_ss, chain_rs,
 ):
     tm = lax.axis_index("tm")
@@ -216,7 +218,6 @@
         middle = 0.5 * (even + odd)
         coarse_end = coarse_ends[spread, :]
         mean[spread, :] = middle - coarse_end
-        jump[spread, :] = middle - coarse_end + first_slice * coarse_end
         half[spread, :] = 0.5 * (even - odd)
 
     def settle_inner(i, carry):
@@ -225,6 +226,49 @@
 
     lax.fori_loop(SUB // 2, CX - SUB // 2, settle_inner, 0, unroll=4)
 
+    jump_parts = ((jump_mid, jumps_mid), (jump_edge, jumps_edge))
+
+    def jump_copy(p, i):
+        source, target = jump_parts[i]
+        return pltpu.make_async_remote_copy(
+            source.at[p], target.at[tm], jump_ss.at[i, p], jump_rs.at[i, tm],
+            device_id=(2 * p, space), device_id_type=MESH,
+        )
+
+    def jump_arrival(n, i):
+        source, target = jump_parts[i]
+        return pltpu.make_async_remote_copy(
+            source.at[0], target.at[n], jump_ss.at[i, 0], jump_rs.at[i, n],
+            device_id=(tm, space), device_id_type=MESH,
+        )
+
+    half_copies = [
+        pltpu.make_async_remote_copy(
+            source, target, half_ss.at[i], half_rs.at[i],
+            device_id=(jnp.minimum(tm + 1, SLICES - 1), space), device_id_type=MESH,
+        )
+        for i, (source, target) in enumerate(((half_mid, prev_mid), (half_edge, prev_edge)))
+    ]
+    passes_on = tm < SLICES - 1
+
+    def sends_to(p):
+        return jnp.logical_and(tm != 2 * p, passes_on)
+
+    for p in range(PLACES):
+        inner = pl.ds(p * CX + 8, MID)
+        jump_mid[p] = mean[inner, :] + first_slice * coarse_ends[inner, :]
+
+        @pl.when(sends_to(p))
+        def _(p=p):
+            jump_copy(p, 0).start()
+
+    for p in range(PLACES):
+        half_mid[p] = half[pl.ds(p * CX + 8, MID), :]
+
+    @pl.when(passes_on)
+    def _():
+        half_copies[0].start()
+
     @pl.when(space > 0)
     def _():
         to_west.wait_send()
@@ -237,56 +281,53 @@
 
     def border(s, carry):
         strength = scale[s]
-        before = west[0, s]
-        now = west[0, s + 1]
+        low, high = carry[:SUB], carry[SUB:]
+        low = low + (west_past[s, 0], west_past[s, 1])
+        high = high + (east_past[s, 0], east_past[s, 1])
+        fresh_low, fresh_high = [], []
         for w in range(SUB):
             at = s + 1 + w
-            after = west[0, at + 1] if w < SUB - 2 else west_past[s, w - (SUB - 2)]
-            west[0, at] = update(
-                before, now, after, west[1, at], west[2, at], west[3, at], strength
+            fresh_low.append(
+                update(
+                    low[w], low[w + 1], low[w + 2],
+                    west[1, at], west[2, at], west[3, at], strength,
+                )
             )
-            before, now = now, after
-        after = east[0, 2 * SUB - 1 - s]
-        now = east[0, 2 * SUB - 2 - s]
-        for w in range(SUB):
             at = 2 * SUB - 2 - s - w
-            before = east[0, at - 1] if w < SUB - 2 else east_past[s, w - (SUB - 2)]
-            east[0, at] = update(
-                before, now, after, east[1, at], east[2, at], east[3, at], strength
+            fresh_high.append(
+                update(
+                    high[w + 2], high[w + 1], high[w],
+                    east[1, at], east[2, at], east[3, at], strength,
+                )
             )
-            after, now = now, before
-        return carry
-
-    lax.fori_loop(0, SUB, border, 0)
+        return tuple(fresh_low) + tuple(fresh_high)
+
+    edge_rows = lax.fori_loop(
+        0, SUB, border,
+        tuple(west[0, w] for w in range(SUB))
+        + tuple(east[0, 2 * SUB - 1 - w] for w in range(SUB)),
+    )
+    low, high = edge_rows[:SUB], edge_rows[SUB:][::-1]
     for i in range(SUB // 2):
-        settle(i, west[0, SUB + 2 * i], west[0, SUB + 2 * i + 1])
-        settle(CX - SUB // 2 + i, east[0, 2 * i], east[0, 2 * i + 1])
-
-    def jump_copy(p):
-        return pltpu.make_async_remote_copy(
-            jump.at[pl.ds(p * CX, CX), :], jumps.at[tm], jump_ss.at[p], jump_rs.at[tm],
-            device_id=(2 * p, space), device_id_type=MESH,
-        )
-
-    def jump_arrival(n):
-        return pltpu.make_async_remote_copy(
-            jump.at[pl.ds(0, CX), :], jumps.at[n], jump_ss.at[0], jump_rs.at[n],
-            device_id=(tm, space), device_id_type=MESH,
-        )
-
-    for p in range(PLACES):
-        @pl.when(jnp.logical_and(tm != 2 * p, tm < SLICES - 1))
+        settle(i, low[2 * i], low[2 * i + 1])
+        settle(CX - SUB // 2 + i, high[2 * i], high[2 * i + 1])
+
+    for p in range(PLACES):
+        for at, first in ((0, 0), (8, CX - 8)):
+            rows = pl.ds(p * CX + first, 8)
+            jump_edge[p, at : at + 8] = mean[rows, :] + first_slice * coarse_ends[rows, :]
+
+        @pl.when(sends_to(p))
         def _(p=p):
-            jump_copy(p).start()
-
-    half_copy = pltpu.make_async_remote_copy(
-        half, half_prev, half_ss, half_rs,
-        device_id=(jnp.minimum(tm + 1, SLICES - 1), space), device_id_type=MESH,
-    )
-
-    @pl.when(tm < SLICES - 1)
-    def _():
-        half_copy.start()
+            jump_copy(p, 1).start()
+
+    for p in range(PLACES):
+        half_edge[p, 0:8] = half[pl.ds(p * CX, 8), :]
+        half_edge[p, 8:16] = half[pl.ds(p * CX + CX - 8, 8), :]
+
+    @pl.when(passes_on)
+    def _():
+        half_copies[1].start()
 
     def state_copy(n):
         return pltpu.make_async_remote_copy(
@@ -302,14 +343,19 @@
 
     @pl.when(is_owner)
     def _():
-        jumps[tm] = jump[pl.ds(pl.multiple_of(chip * CX, CX), CX), :]
+        jumps_mid[tm] = jump_mid[chip]
+        jumps_edge[tm] = jump_edge[chip]
 
         def link(n, values):
             @pl.when(n != tm)
             def _():
-                jump_arrival(n).wait_recv()
-
-            values = jumps[n] + jnp.where(n > 0, 1.0, 0.0) * apply_coarse(chip, values)
+                for i in range(2):
+                    jump_arrival(n, i).wait_recv()
+
+            own = jnp.concatenate(
+                [jumps_edge[n, 0:8], jumps_mid[n], jumps_edge[n, 8:16]], axis=0
+            )
+            values = own + jnp.where(n > 0, 1.0, 0.0) * apply_coarse(chip, values)
             chain[n + 1] = values
 
             @pl.when(n + 1 != tm)
@@ -343,21 +389,27 @@
 
     @pl.when(tm > 0)
     def _():
-        half_copy.wait_recv()
-        prev_out[...] = half_prev[...]
+        for copy in half_copies:
+            copy.wait_recv()
+        for p in range(PLACES):
+            prev_out[pl.ds(p * CX, 8), :] = prev_edge[p, 0:8]
+            prev_out[pl.ds(p * CX + 8, MID), :] = prev_mid[p]
+            prev_out[pl.ds(p * CX + CX - 8, 8), :] = prev_edge[p, 8:16]
 
     @pl.when(tm == 0)
     def _():
         prev_out[...] = jnp.zeros_like(prev_out)
 
     for p in range(PLACES):
-        @pl.when(jnp.logical_and(tm != 2 * p, tm < SLICES - 1))
+        @pl.when(sends_to(p))
         def _(p=p):
-            jump_copy(p).wait_send()
-
-    @pl.when(tm < SLICES - 1)
-    def _():
-        half_copy.wait_send()
+            for i in range(2):
+                jump_copy(p, i).wait_send()
+
+    @pl.when(passes_on)
+    def _():
+        for copy in half_copies:
+            copy.wait_send()
 
     @pl.when(is_owner)
     def _():
@@ -371,20 +423,46 @@
         lax.fori_loop(1, SLICES, sent, 0)
 
 
-def finish_kernel(neighbors, starts, sums, coarse, half, prev, ends_out, step_out):
+def finish_kernel(
+    neighbors, starts_hbm, sums_hbm, coarse_hbm, half_hbm, prev_hbm, ends_hbm, step_hbm,
+    starts, sums, coarse, half, prev, ends, step, load_sem, store_sem,
+):
+    loads = [
+        pltpu.make_async_copy(src, dst, load_sem.at[i])
+        for i, (src, dst) in enumerate(
+            [(sums_hbm, sums), (half_hbm, half), (coarse_hbm, coarse), (prev_hbm, prev),
+             (starts_hbm, starts)]
+        )
+    ]
+    for load in loads:
+        load.start()
     tm = lax.axis_index("tm")
     order = place_order(neighbors, lax.axis_index("space"))
     later = jnp.where(tm > 0, 1.0, 0.0)
+    even, odd = pl.ds(0, CX, stride=2), pl.ds(1, CX, stride=2)
+    loads[0].wait()
+    loads[1].wait()
+    stores = []
     for p in range(PLACES):
         t = order[p]
         rows = pl.ds(p * CX, CX)
-        even, odd = pl.ds(0, CX, stride=2), pl.ds(1, CX, stride=2)
         total, difference = sums[rows, :], half[rows, :]
-        ends_out[t, even, :] = total + difference
-        ends_out[t, odd, :] = total - difference
+        ends[p, even, :] = total + difference
+        ends[p, odd, :] = total - difference
+        stores.append(pltpu.make_async_copy(ends.at[p], ends_hbm.at[t], store_sem.at[0, p]))
+        stores[-1].start()
+    for load in loads[2:]:
+        load.wait()
+    for p in range(PLACES):
+        t = order[p]
+        rows = pl.ds(p * CX, CX)
         total, difference = coarse[rows, :], prev[rows, :]
-        step_out[t, even, :] = later * (total + difference - starts[t, even, :])
-        step_out[t, odd, :] = later * (total - difference - starts[t, odd, :])
+        step[p, even, :] = later * (total + difference - starts[t, even, :])
+        step[p, odd, :] = later * (total - difference - starts[t, odd, :])
+        stores.append(pltpu.make_async_copy(step.at[p], step_hbm.at[t], store_sem.at[1, p]))
+        stores[-1].start()
+    for store in stores:
+        store.wait()
 
 
 def on_device(
@@ -397,6 +475,7 @@
     places = jax.ShapeDtypeStruct((PLACES * CX, TILE), F32)
     dma = pltpu.SemaphoreType.DMA
     starts = starts[0]
+    neighbors = neighbors.T
     sums, coarse, half, prev = pl.pallas_call(
         fine_kernel,
         out_shape=(places,) * 4,
@@ -426,17 +505,22 @@
             pltpu.VMEM((PLACES * CX, TILE), F32),
             pltpu.VMEM((PLACES * CX, TILE), F32),
             pltpu.VMEM((PLACES * CX, TILE), F32),
-            pltpu.VMEM((PLACES * CX, TILE), F32),
-            pltpu.VMEM((PLACES * CX, TILE), F32),
-            pltpu.VMEM((SLICES, CX, TILE), F32),
+            pltpu.VMEM((PLACES, MID, TILE), F32),
+            pltpu.VMEM((PLACES, 16, TILE), F32),
+            pltpu.VMEM((PLACES, MID, TILE), F32),
+            pltpu.VMEM((PLACES, 16, TILE), F32),
+            pltpu.VMEM((PLACES, MID, TILE), F32),
+            pltpu.VMEM((PLACES, 16, TILE), F32),
+            pltpu.VMEM((SLICES, MID, TILE), F32),
+            pltpu.VMEM((SLICES, 16, TILE), F32),
             pltpu.VMEM((SLICES, CX, TILE), F32),
             pltpu.VMEM((PLACES, CX, TILE), F32),
             dma((2,)),
             dma((2,)),
-            dma((PLACES,)),
-            dma((SLICES,)),
-            dma,
-            dma,
+            dma((2, PLACES)),
+            dma((2, SLICES)),
+            dma((2,)),
+            dma((2,)),
             dma((SLICES,)),
             dma((PLACES,)),
         ],
@@ -447,9 +531,13 @@
     ends, step = pl.pallas_call(
         finish_kernel,
         out_shape=(jax.ShapeDtypeStruct(tiles, F32),) * 2,
-        in_specs=[smem] + [vmem] * 5,
-        out_specs=(vmem, vmem),
-        compiler_params=pltpu.CompilerParams(vmem_limit_bytes=40 << 20),
+        in_specs=[smem] + [anywhere] * 5,
+        out_specs=(anywhere, anywhere),
+        scratch_shapes=[pltpu.VMEM(tiles, F32)]
+        + [pltpu.VMEM((PLACES * CX, TILE), F32)] * 4
+        + [pltpu.VMEM(tiles, F32)] * 2
+        + [dma((5,)), dma((2, PLACES))],
+        compiler_params=pltpu.CompilerParams(vmem_limit_bytes=60 << 20),
     )(neighbors, starts, sums, coarse, half, prev)
     return ends[None], step[None]
 

time: 46.3 us -> 38.3 us (0.83)
  the two profiles are of different devices: /device:TPU:27 before, /device:TPU:121 now
where the time goes in v2:
time: 38.3 us; the launch traced here: 38.1 us
  Pallas kernels  37.4 us (98%)
  between operations  0.64 us (2%)
    pallas_call x1, Pallas kernels, on_device(): pl.pallas_call(fine_kernel, out_shape=(places,) * 4, in_specs=[smem, smem...  34.4 us
    pallas_call x1, Pallas kernels, on_device(): pl.pallas_call(finish_kernel, out_shape=(jax.ShapeDtypeStruct(tiles, F32)...  3.03 us

profile of v2, /device:TPU:121, one launch (start us, length us, event | category | flops | bytes accessed | tf_op | source)
XLA Modules:
  0.0 38.1 jit_solution(3733239134718618544)
XLA Ops:
  0.6 34.4 %shard_map.95 = (f32[512,128]{1,0:T(8,128)}, f32[512,128]{1,0:T(8,128)}, f32[512,128]{1,0:T(8,128)}, f32[512,128]{1,0:T(8,128)}) custom-call(f32[12]{0:T(128)} %scale.1, s32[4,8]{1,0:T(4,128)} %bitcast.6, f32[8,128,128]{2,1,0:T(8,128)} %bitcast.4, f32[8,128,128]{2,1,0:T(8,128)} %diff_hbm.1, f32[2,8,128,128]{3,2,1,0:T(8,128)} %vel_hbm.1, ...), custom_call_target="tpu_custom_call" | custom-call | tf_op jit(solution)/shard_map/pallas_call | solution.py:479
  35.1 3.0 %shard_map.96 = (f32[8,128,128]{2,1,0:T(8,128)}, f32[8,128,128]{2,1,0:T(8,128)}) custom-call(s32[4,8]{1,0:T(4,128)} %bitcast.7, f32[8,128,128]{2,1,0:T(8,128)} %bitcast.5, f32[512,128]{1,0:T(8,128)} %get-tuple-element.8.sums_hbm, f32[512,128]{1,0:T(8,128)} %get-tuple-element.9.coarse_hbm, f32[512,128]{1,0:T(8,128)} %get-tuple-element.10.half_hbm, ...), custom_call_target="tpu_custom_call" | custom-call | tf_op jit(solution)/shard_map/pallas_call | solution.py:531

commit v3 on v2

--- a/solution.py
+++ b/solution.py
@@ -12,7 +12,6 @@
 CX = 64
 MID = 48
 SLICES = 16
-BLOCK = 32
 F32 = jnp.float32
 BF16 = jnp.bfloat16
 
@@ -42,13 +41,14 @@
 
 
 def fine_kernel(
-    scale, neighbors, starts_hbm, diff_hbm, vel_hbm, obst_hbm, cx_hbm, cy_hbm,
+    scale_hbm, neighbors_hbm, starts_hbm, diff_hbm, vel_hbm, obst_hbm, cx_hbm, cy_hbm,
     sum_out, coarse_out, half_out, prev_out,
-    starts, diff, vel, obst, cx, cy, load_sem,
+    scale, neighbors, starts_edge, diff_edge, vel_edge, obst_edge, starts, diff, vel, obst,
+    cx, cy, load_sem, store_sem,
     state, coef_d, coef_a, coef_b, west, east, west_past, east_past,
     xh, xl, yh, yl, coarse_starts, coarse_ends, mean, half,
     jump_mid, jump_edge, half_mid, half_edge, prev_mid, prev_edge, jumps_mid, jumps_edge,
-    chain, coarse,
+    chain, coarse, sums,
     halo_ss, halo_rs, jump_ss, jump_rs, half_ss, half_rs, chain_ss, chain_rs,
 ):
     tm = lax.axis_index("tm")
@@ -57,12 +57,21 @@
     chip = tm // 2
     is_owner = core == 0
 
+    fields = (starts_hbm, diff_hbm, obst_hbm, vel_hbm)
+    edges = (starts_edge, diff_edge, obst_edge, vel_edge)
+    inner = (starts, diff, obst, vel)
+    pairs = [(neighbors_hbm, neighbors), (scale_hbm, scale)]
+    for first, at in ((0, 0), (TILE - 16, 16)):
+        pairs += [
+            (src.at[..., pl.ds(first, 16), :], dst.at[..., pl.ds(at, 16), :])
+            for src, dst in zip(fields, edges)
+        ]
+    pairs += [
+        (src.at[..., pl.ds(16, TILE - 32), :], dst) for src, dst in zip(fields, inner)
+    ]
+    pairs += [(cx_hbm, cx), (cy_hbm, cy)]
     loads = [
-        pltpu.make_async_copy(src, dst, load_sem.at[i])
-        for i, (src, dst) in enumerate(
-            [(starts_hbm, starts), (diff_hbm, diff), (obst_hbm, obst), (vel_hbm, vel),
-             (cx_hbm, cx), (cy_hbm, cy)]
-        )
+        pltpu.make_async_copy(src, dst, load_sem.at[i]) for i, (src, dst) in enumerate(pairs)
     ]
     for load in loads:
         load.start()
@@ -88,30 +97,28 @@
 
     lax.fori_loop(1, SLICES, greet_slice, 0)
 
+    def convert(p, block, at, sources):
+        first, diffusion, tubes, speed = sources
+        rows = pl.ds(at if isinstance(at, int) else pl.multiple_of(at, 8), 8)
+        spread = pl.ds(block * 64 + p, 8, stride=8)
+        t = order[p]
+        open_cells = 1.0 - tubes[t, rows, :].astype(F32)
+        state[spread, :] = first[t, rows, :]
+        coef_d[spread, :] = open_cells * diffusion[t, rows, :]
+        coef_a[spread, :] = (0.5 * open_cells) * speed[0, t, rows, :]
+        coef_b[spread, :] = (0.5 * open_cells) * speed[1, t, rows, :]
+
+    for load in loads[:10]:
+        load.wait()
     order = place_order(neighbors, space)
-
-    for load in loads[:4]:
-        load.wait()
-    for p in range(PLACES):
-        t = order[p]
-
-        def convert(i, carry):
-            rows = pl.ds(pl.multiple_of(i * 8, 8), 8)
-            spread = pl.ds(i * 64 + p, 8, stride=8)
-            open_cells = 1.0 - obst[t, rows, :].astype(F32)
-            state[spread, :] = starts[t, rows, :]
-            coef_d[spread, :] = open_cells * diff[t, rows, :]
-            coef_a[spread, :] = (0.5 * open_cells) * vel[0, t, rows, :]
-            coef_b[spread, :] = (0.5 * open_cells) * vel[1, t, rows, :]
-            return carry
-
-        lax.fori_loop(0, TILE // 8, convert, 0, unroll=4)
+    for p in range(PLACES):
+        for i, block in enumerate((0, 1, TILE // 8 - 2, TILE // 8 - 1)):
+            convert(p, block, 8 * i, edges)
 
     def row(ref, r):
         at = r * 8 if isinstance(r, int) else pl.multiple_of(r * 8, 8)
         return ref[pl.ds(at, 8), :]
 
-    state[pl.ds(TILE * 8, 8), :] = jnp.zeros((8, TILE), F32)
     for q, ref in enumerate((state, coef_d, coef_a, coef_b)):
         for i in range(SUB):
             west[q, SUB + i] = row(ref, i)
@@ -126,7 +133,6 @@
         east[:, SUB : 2 * SUB] = jnp.zeros((4, SUB, 8, TILE), F32)
 
     greeted = SLICES - 1 + jnp.where(space > 0, 1, 0) + jnp.where(space < 7, 1, 0)
-    pl.semaphore_wait(barrier, greeted)
 
     to_west = pltpu.make_async_remote_copy(
         west.at[:, SUB : 2 * SUB], east.at[:, SUB : 2 * SUB], halo_ss.at[0], halo_rs.at[1],
@@ -137,36 +143,42 @@
         device_id=(tm, jnp.minimum(space + 1, 7)), device_id_type=MESH,
     )
 
-    @pl.when(space > 0)
-    def _():
-        to_west.start()
-
-    @pl.when(space < 7)
-    def _():
-        to_east.start()
-
     lane = lax.broadcasted_iota(jnp.int32, (8, TILE), 1)
     sub = lax.broadcasted_iota(jnp.int32, (8, TILE), 0)
     south_face = lane == 0
     north_face = lane == TILE - 1
-    south_end = jnp.logical_and(south_face, sub == 0)
-    north_end = jnp.logical_and(north_face, sub == 7)
+    north_wrap = jnp.logical_and(north_face, sub == 0)
+    south_wrap = jnp.logical_and(south_face, sub == 7)
 
     def update(before, now, after, d, a, b, strength):
-        south = pltpu.roll(now, 1, 1)
-        south = jnp.where(south_face, pltpu.roll(south, 1, 0), south)
-        south = jnp.where(south_end, 0.0, south)
-        north = pltpu.roll(now, TILE - 1, 1)
-        north = jnp.where(north_face, pltpu.roll(north, 7, 0), north)
-        north = jnp.where(north_end, 0.0, north)
+        south = jnp.where(north_face, pltpu.roll(now, 1, 0), now)
+        south = pltpu.roll(jnp.where(north_wrap, 0.0, south), 1, 1)
+        north = jnp.where(south_face, pltpu.roll(now, 7, 0), now)
+        north = pltpu.roll(jnp.where(south_wrap, 0.0, north), TILE - 1, 1)
         laplace = (before + after) + (south + north) - 4.0 * now
-        kept = jnp.where(d > 0.0, now, 0.0)
-        return (
-            kept + (strength * d) * laplace - a * (after - before) - b * (north - south)
-        )
-
-    for load in loads[4:]:
+        return now + (strength * d) * laplace - a * (after - before) - b * (north - south)
+
+    pl.semaphore_wait(barrier, greeted)
+
+    @pl.when(space > 0)
+    def _():
+        to_west.start()
+
+    @pl.when(space < 7)
+    def _():
+        to_east.start()
+
+    for load in loads[10:]:
         load.wait()
+    state[pl.ds(TILE * 8, 8), :] = jnp.zeros((8, TILE), F32)
+    for p in range(PLACES):
+
+        def convert_inner(i, carry, p=p):
+            convert(p, i + 2, i * 8, inner)
+            return carry
+
+        lax.fori_loop(0, TILE // 8 - 4, convert_inner, 0, unroll=4)
+
     for p in range(PLACES):
         t = order[p]
         x_high, x_low = halves(cx[t])
@@ -175,9 +187,15 @@
         y_high, y_low = halves(cy[t].T)
         yh[p] = y_high
         yl[p] = y_low
-        coarse_starts[p] = 0.5 * (
-            starts[t, pl.ds(0, CX, stride=2), :] + starts[t, pl.ds(1, CX, stride=2), :]
-        )
+        for ref, at, target in (
+            (starts_edge, 0, slice(0, 8)),
+            (starts_edge, 16, slice(CX - 8, CX)),
+            (starts, 0, slice(8, CX - 8)),
+        ):
+            count = target.stop - target.start
+            coarse_starts[p, target] = 0.5 * (
+                ref[t, pl.ds(at, count, stride=2), :] + ref[t, pl.ds(at + 1, count, stride=2), :]
+            )
 
     def apply_coarse(p, values):
         mixed = product((xh[p], xl[p]), halves(values))
@@ -192,21 +210,21 @@
         west_past[s, 1] = row(state, s + 1)
         east_past[s, 0] = row(state, TILE - 1 - s)
         east_past[s, 1] = row(state, TILE - 2 - s)
-
-        def rows(i, before):
-            base = i * BLOCK
-            now = row(state, base)
-            for r in range(BLOCK):
-                at = base + r
-                after = row(state, at + 1)
-                fresh = update(
-                    before, now, after, row(coef_d, at), row(coef_a, at), row(coef_b, at), strength
-                )
-                state[pl.ds(pl.multiple_of(at * 8, 8), 8), :] = fresh
-                before, now = now, after
-            return before
-
-        lax.fori_loop(0, TILE // BLOCK, rows, jnp.zeros((8, TILE), F32))
+        before = jnp.zeros((8, TILE), F32)
+        now = row(state, 0)
+        for r in range(TILE):
+            after = row(state, r + 1)
+            state[r * 8 : r * 8 + 8, :] = update(
+                before, now, after, row(coef_d, r), row(coef_a, r), row(coef_b, r), strength
+            )
+            before, now = now, after
+
+        @pl.when(s == 0)
+        def _():
+            for r in range(TILE):
+                here = slice(r * 8, r * 8 + 8)
+                state[here, :] = jnp.where(coef_d[here, :] > 0.0, state[here, :], 0.0)
+
         return carry
 
     lax.fori_loop(0, SUB, substep, 0)
@@ -255,8 +273,8 @@
         return jnp.logical_and(tm != 2 * p, passes_on)
 
     for p in range(PLACES):
-        inner = pl.ds(p * CX + 8, MID)
-        jump_mid[p] = mean[inner, :] + first_slice * coarse_ends[inner, :]
+        rows = pl.ds(p * CX + 8, MID)
+        jump_mid[p] = mean[rows, :] + first_slice * coarse_ends[rows, :]
 
         @pl.when(sends_to(p))
         def _(p=p):
@@ -287,19 +305,15 @@
         fresh_low, fresh_high = [], []
         for w in range(SUB):
             at = s + 1 + w
-            fresh_low.append(
-                update(
-                    low[w], low[w + 1], low[w + 2],
-                    west[1, at], west[2, at], west[3, at], strength,
-                )
+            fresh = update(
+                low[w], low[w + 1], low[w + 2], west[1, at], west[2, at], west[3, at], strength
             )
+            fresh_low.append(jnp.where(west[1, at] > 0.0, fresh, 0.0))
             at = 2 * SUB - 2 - s - w
-            fresh_high.append(
-                update(
-                    high[w + 2], high[w + 1], high[w],
-                    east[1, at], east[2, at], east[3, at], strength,
-                )
+            fresh = update(
+                high[w + 2], high[w + 1], high[w], east[1, at], east[2, at], east[3, at], strength
             )
+            fresh_high.append(jnp.where(east[1, at] > 0.0, fresh, 0.0))
         return tuple(fresh_low) + tuple(fresh_high)
 
     edge_rows = lax.fori_loop(
@@ -374,31 +388,42 @@
     def _():
         coarse[...] = coarse_starts[...]
 
-    half_out[...] = half[...]
-
-    for p in range(PLACES):
-        remote = jnp.logical_and(tm > 0, tm != 2 * p)
-
-        @pl.when(remote)
+    stores = [
+        pltpu.make_async_copy(half.at[pl.ds(p * CX, CX), :], half_out.at[p], store_sem.at[0, p])
+        for p in range(PLACES)
+    ]
+    for store in stores:
+        store.start()
+
+    for p in range(PLACES):
+        @pl.when(jnp.logical_and(tm > 0, tm != 2 * p))
         def _(p=p):
             state_arrival(p).wait_recv()
 
-        values = coarse[p]
-        coarse_out[pl.ds(p * CX, CX), :] = values
-        sum_out[pl.ds(p * CX, CX), :] = apply_coarse(p, values) + mean[pl.ds(p * CX, CX), :]
+        stores.append(pltpu.make_async_copy(coarse.at[p], coarse_out.at[p], store_sem.at[1, p]))
+        stores[-1].start()
+        sums[p] = apply_coarse(p, coarse[p]) + mean[pl.ds(p * CX, CX), :]
+        stores.append(pltpu.make_async_copy(sums.at[p], sum_out.at[p], store_sem.at[2, p]))
+        stores[-1].start()
 
     @pl.when(tm > 0)
     def _():
         for copy in half_copies:
             copy.wait_recv()
-        for p in range(PLACES):
-            prev_out[pl.ds(p * CX, 8), :] = prev_edge[p, 0:8]
-            prev_out[pl.ds(p * CX + 8, MID), :] = prev_mid[p]
-            prev_out[pl.ds(p * CX + CX - 8, 8), :] = prev_edge[p, 8:16]
-
-    @pl.when(tm == 0)
-    def _():
-        prev_out[...] = jnp.zeros_like(prev_out)
+        prev_stores = [
+            pltpu.make_async_copy(src, prev_out.at[:, rows, :], store_sem.at[3, i])
+            for i, (src, rows) in enumerate(
+                [(prev_mid, pl.ds(8, MID)), (prev_edge.at[:, 0:8], pl.ds(0, 8)),
+                 (prev_edge.at[:, 8:16], pl.ds(CX - 8, 8))]
+            )
+        ]
+        for store in prev_stores:
+            store.start()
+        for store in prev_stores:
+            store.wait()
+
+    for store in stores:
+        store.wait()
 
     for p in range(PLACES):
         @pl.when(sends_to(p))
@@ -424,41 +449,38 @@
 
 
 def finish_kernel(
-    neighbors, starts_hbm, sums_hbm, coarse_hbm, half_hbm, prev_hbm, ends_hbm, step_hbm,
-    starts, sums, coarse, half, prev, ends, step, load_sem, store_sem,
+    neighbors_hbm, starts_hbm, sums_hbm, coarse_hbm, half_hbm, prev_hbm, ends_hbm, step_hbm,
+    neighbors, starts, sums, coarse, half, prev, ends, step, load_sem, store_sem,
 ):
     loads = [
         pltpu.make_async_copy(src, dst, load_sem.at[i])
         for i, (src, dst) in enumerate(
-            [(sums_hbm, sums), (half_hbm, half), (coarse_hbm, coarse), (prev_hbm, prev),
-             (starts_hbm, starts)]
+            [(neighbors_hbm, neighbors), (sums_hbm, sums), (half_hbm, half),
+             (coarse_hbm, coarse), (prev_hbm, prev), (starts_hbm, starts)]
         )
     ]
     for load in loads:
         load.start()
-    tm = lax.axis_index("tm")
+    later = lax.axis_index("tm") > 0
+    even, odd = pl.ds(0, CX, stride=2), pl.ds(1, CX, stride=2)
+    for load in loads[:3]:
+        load.wait()
     order = place_order(neighbors, lax.axis_index("space"))
-    later = jnp.where(tm > 0, 1.0, 0.0)
-    even, odd = pl.ds(0, CX, stride=2), pl.ds(1, CX, stride=2)
-    loads[0].wait()
-    loads[1].wait()
     stores = []
     for p in range(PLACES):
         t = order[p]
-        rows = pl.ds(p * CX, CX)
-        total, difference = sums[rows, :], half[rows, :]
+        total, difference = sums[p], half[p]
         ends[p, even, :] = total + difference
         ends[p, odd, :] = total - difference
         stores.append(pltpu.make_async_copy(ends.at[p], ends_hbm.at[t], store_sem.at[0, p]))
         stores[-1].start()
-    for load in loads[2:]:
+    for load in loads[3:]:
         load.wait()
     for p in range(PLACES):
         t = order[p]
-        rows = pl.ds(p * CX, CX)
-        total, difference = coarse[rows, :], prev[rows, :]
-        step[p, even, :] = later * (total + difference - starts[t, even, :])
-        step[p, odd, :] = later * (total - difference - starts[t, odd, :])
+        total, difference = coarse[p], prev[p]
+        step[p, even, :] = jnp.where(later, total + difference - starts[t, even, :], 0.0)
+        step[p, odd, :] = jnp.where(later, total - difference - starts[t, odd, :], 0.0)
         stores.append(pltpu.make_async_copy(step.at[p], step_hbm.at[t], store_sem.at[1, p]))
         stores[-1].start()
     for store in stores:
@@ -468,27 +490,32 @@
 def on_device(
     starts, diffusivity, velocity, obstacle, substep_scale, neighbors, coarse_x, coarse_y
 ):
-    smem = pl.BlockSpec(memory_space=pltpu.SMEM)
-    vmem = pl.BlockSpec(memory_space=pltpu.VMEM)
     anywhere = pl.BlockSpec(memory_space=pl.ANY)
     tiles = (PLACES, TILE, TILE)
-    places = jax.ShapeDtypeStruct((PLACES * CX, TILE), F32)
+    places = jax.ShapeDtypeStruct((PLACES, CX, TILE), F32)
     dma = pltpu.SemaphoreType.DMA
     starts = starts[0]
     neighbors = neighbors.T
     sums, coarse, half, prev = pl.pallas_call(
         fine_kernel,
         out_shape=(places,) * 4,
-        in_specs=[smem, smem] + [anywhere] * 6,
-        out_specs=(vmem,) * 4,
+        in_specs=[anywhere] * 8,
+        out_specs=(anywhere,) * 4,
         scratch_shapes=[
-            pltpu.VMEM(tiles, F32),
-            pltpu.VMEM(tiles, F32),
-            pltpu.VMEM((2,) + tiles, F32),
-            pltpu.VMEM(tiles, jnp.int32),
+            pltpu.SMEM((SUB,), F32),
+            pltpu.SMEM((4, PLACES), jnp.int32),
+            pltpu.VMEM((PLACES, 32, TILE), F32),
+            pltpu.VMEM((PLACES, 32, TILE), F32),
+            pltpu.VMEM((2, PLACES, 32, TILE), F32),
+            pltpu.VMEM((PLACES, 32, TILE), jnp.int32),
+            pltpu.VMEM((PLACES, TILE - 32, TILE), F32),
+            pltpu.VMEM((PLACES, TILE - 32, TILE), F32),
+            pltpu.VMEM((2, PLACES, TILE - 32, TILE), F32),
+            pltpu.VMEM((PLACES, TILE - 32, TILE), jnp.int32),
             pltpu.VMEM((PLACES, CX, CX), F32),
             pltpu.VMEM(tiles, F32),
-            dma((6,)),
+            dma((16,)),
+            dma((4, PLACES)),
             pltpu.VMEM((TILE * 8 + 8, TILE), F32),
             pltpu.VMEM((TILE * 8, TILE), F32),
             pltpu.VMEM((TILE * 8, TILE), F32),
@@ -515,6 +542,7 @@
             pltpu.VMEM((SLICES, 16, TILE), F32),
             pltpu.VMEM((SLICES, CX, TILE), F32),
             pltpu.VMEM((PLACES, CX, TILE), F32),
+            pltpu.VMEM((PLACES, CX, TILE), F32),
             dma((2,)),
             dma((2,)),
             dma((2, PLACES)),
@@ -531,12 +559,12 @@
     ends, step = pl.pallas_call(
         finish_kernel,
         out_shape=(jax.ShapeDtypeStruct(tiles, F32),) * 2,
-        in_specs=[smem] + [anywhere] * 5,
+        in_specs=[anywhere] * 6,
         out_specs=(anywhere, anywhere),
-        scratch_shapes=[pltpu.VMEM(tiles, F32)]
-        + [pltpu.VMEM((PLACES * CX, TILE), F32)] * 4
+        scratch_shapes=[pltpu.SMEM((4, PLACES), jnp.int32), pltpu.VMEM(tiles, F32)]
+        + [pltpu.VMEM((PLACES, CX, TILE), F32)] * 4
         + [pltpu.VMEM(tiles, F32)] * 2
-        + [dma((5,)), dma((2, PLACES))],
+        + [dma((6,)), dma((2, PLACES))],
         compiler_params=pltpu.CompilerParams(vmem_limit_bytes=60 << 20),
     )(neighbors, starts, sums, coarse, half, prev)
     return ends[None], step[None]

time: 38.3 us -> 34.8 us (0.909)
  the two profiles are of different devices: /device:TPU:121 before, /device:TPU:27 now
where the time goes in v3:
time: 34.8 us; the launch traced here: 34.7 us
  Pallas kernels  34.1 us (98%)
  between operations  0.64 us (2%)
    pallas_call x1, Pallas kernels, on_device(): pl.pallas_call(fine_kernel, out_shape=(places,) * 4, in_specs=[anywhere]...  31.7 us
    pallas_call x1, Pallas kernels, on_device(): pl.pallas_call(finish_kernel, out_shape=(jax.ShapeDtypeStruct(tiles, F32)...  2.35 us

profile of v3, /device:TPU:27, one launch (start us, length us, event | category | flops | bytes accessed | tf_op | source)
XLA Modules:
  0.0 34.7 jit_solution(15495251026488266077)
XLA Ops:
  0.6 31.7 %shard_map.95 = (f32[8,64,128]{2,1,0:T(8,128)}, f32[8,64,128]{2,1,0:T(8,128)}, f32[8,64,128]{2,1,0:T(8,128)}, f32[8,64,128]{2,1,0:T(8,128)}) custom-call(f32[12]{0:T(128)} %scale_hbm.1, s32[4,8]{1,0:T(4,128)} %bitcast.6, f32[8,128,128]{2,1,0:T(8,128)} %bitcast.4, f32[8,128,128]{2,1,0:T(8,128)} %diff_hbm.1, f32[2,8,128,128]{3,2,1,0:T(8,128)} %vel_hbm.1, ...), custom_call_target="tpu_custom_call" | custom-call | tf_op jit(solution)/shard_map/pallas_call | solution.py:499
  32.3 2.3 %shard_map.96 = (f32[8,128,128]{2,1,0:T(8,128)}, f32[8,128,128]{2,1,0:T(8,128)}) custom-call(s32[4,8]{1,0:T(4,128)} %bitcast.7, f32[8,128,128]{2,1,0:T(8,128)} %bitcast.5, f32[8,64,128]{2,1,0:T(8,128)} %get-tuple-element.8.sums_hbm, f32[8,64,128]{2,1,0:T(8,128)} %get-tuple-element.9.coarse_hbm, f32[8,64,128]{2,1,0:T(8,128)} %get-tuple-element.10.half_hbm, ...), custom_call_target="tpu_custom_call" | custom-call | tf_op jit(solution)/shard_map/pallas_call | solution.py:559

commit v4 on v3

--- a/solution.py
+++ b/solution.py
@@ -44,11 +44,11 @@
     scale_hbm, neighbors_hbm, starts_hbm, diff_hbm, vel_hbm, obst_hbm, cx_hbm, cy_hbm,
     sum_out, coarse_out, half_out, prev_out,
     scale, neighbors, starts_edge, diff_edge, vel_edge, obst_edge, starts, diff, vel, obst,
-    cx, cy, load_sem, store_sem,
+    cx, cy, load_sem,
     state, coef_d, coef_a, coef_b, west, east, west_past, east_past,
     xh, xl, yh, yl, coarse_starts, coarse_ends, mean, half,
     jump_mid, jump_edge, half_mid, half_edge, prev_mid, prev_edge, jumps_mid, jumps_edge,
-    chain, coarse, sums,
+    chain, coarse,
     halo_ss, halo_rs, jump_ss, jump_rs, half_ss, half_rs, chain_ss, chain_rs,
 ):
     tm = lax.axis_index("tm")
@@ -388,42 +388,26 @@
     def _():
         coarse[...] = coarse_starts[...]
 
-    stores = [
-        pltpu.make_async_copy(half.at[pl.ds(p * CX, CX), :], half_out.at[p], store_sem.at[0, p])
-        for p in range(PLACES)
-    ]
-    for store in stores:
-        store.start()
+    for p in range(PLACES):
+        half_out[p] = half[pl.ds(p * CX, CX), :]
 
     for p in range(PLACES):
         @pl.when(jnp.logical_and(tm > 0, tm != 2 * p))
         def _(p=p):
             state_arrival(p).wait_recv()
 
-        stores.append(pltpu.make_async_copy(coarse.at[p], coarse_out.at[p], store_sem.at[1, p]))
-        stores[-1].start()
-        sums[p] = apply_coarse(p, coarse[p]) + mean[pl.ds(p * CX, CX), :]
-        stores.append(pltpu.make_async_copy(sums.at[p], sum_out.at[p], store_sem.at[2, p]))
-        stores[-1].start()
+        values = coarse[p]
+        coarse_out[p] = values
+        sum_out[p] = apply_coarse(p, values) + mean[pl.ds(p * CX, CX), :]
 
     @pl.when(tm > 0)
     def _():
         for copy in half_copies:
             copy.wait_recv()
-        prev_stores = [
-            pltpu.make_async_copy(src, prev_out.at[:, rows, :], store_sem.at[3, i])
-            for i, (src, rows) in enumerate(
-                [(prev_mid, pl.ds(8, MID)), (prev_edge.at[:, 0:8], pl.ds(0, 8)),
-                 (prev_edge.at[:, 8:16], pl.ds(CX - 8, 8))]
-            )
-        ]
-        for store in prev_stores:
-            store.start()
-        for store in prev_stores:
-            store.wait()
-
-    for store in stores:
-        store.wait()
+        for p in range(PLACES):
+            prev_out[p, 0:8] = prev_edge[p, 0:8]
+            prev_out[p, 8 : CX - 8] = prev_mid[p]
+            prev_out[p, CX - 8 : CX] = prev_edge[p, 8:16]
 
     for p in range(PLACES):
         @pl.when(sends_to(p))
@@ -449,22 +433,20 @@
 
 
 def finish_kernel(
-    neighbors_hbm, starts_hbm, sums_hbm, coarse_hbm, half_hbm, prev_hbm, ends_hbm, step_hbm,
-    neighbors, starts, sums, coarse, half, prev, ends, step, load_sem, store_sem,
+    neighbors_hbm, starts_hbm, sums, coarse, half, prev, ends_hbm, step_hbm,
+    neighbors, starts, ends, step, load_sem, store_sem,
 ):
     loads = [
         pltpu.make_async_copy(src, dst, load_sem.at[i])
         for i, (src, dst) in enumerate(
-            [(neighbors_hbm, neighbors), (sums_hbm, sums), (half_hbm, half),
-             (coarse_hbm, coarse), (prev_hbm, prev), (starts_hbm, starts)]
+            [(neighbors_hbm, neighbors), (starts_hbm, starts)]
         )
     ]
     for load in loads:
         load.start()
     later = lax.axis_index("tm") > 0
     even, odd = pl.ds(0, CX, stride=2), pl.ds(1, CX, stride=2)
-    for load in loads[:3]:
-        load.wait()
+    loads[0].wait()
     order = place_order(neighbors, lax.axis_index("space"))
     stores = []
     for p in range(PLACES):
@@ -474,8 +456,7 @@
         ends[p, odd, :] = total - difference
         stores.append(pltpu.make_async_copy(ends.at[p], ends_hbm.at[t], store_sem.at[0, p]))
         stores[-1].start()
-    for load in loads[3:]:
-        load.wait()
+    loads[1].wait()
     for p in range(PLACES):
         t = order[p]
         total, difference = coarse[p], prev[p]
@@ -490,17 +471,19 @@
 def on_device(
     starts, diffusivity, velocity, obstacle, substep_scale, neighbors, coarse_x, coarse_y
 ):
-    anywhere = pl.BlockSpec(memory_space=pl.ANY)
+    anywhere = pl.BlockSpec(memory_space=pltpu.HBM)
+    vmem = pl.BlockSpec(memory_space=pltpu.VMEM)
     tiles = (PLACES, TILE, TILE)
-    places = jax.ShapeDtypeStruct((PLACES, CX, TILE), F32)
+    places = pltpu.VMEM((PLACES, CX, TILE), F32)
     dma = pltpu.SemaphoreType.DMA
     starts = starts[0]
+    in_hbm = lambda x: pltpu.with_memory_space_constraint(x, pltpu.HBM)
     neighbors = neighbors.T
     sums, coarse, half, prev = pl.pallas_call(
         fine_kernel,
         out_shape=(places,) * 4,
         in_specs=[anywhere] * 8,
-        out_specs=(anywhere,) * 4,
+        out_specs=(vmem,) * 4,
         scratch_shapes=[
             pltpu.SMEM((SUB,), F32),
             pltpu.SMEM((4, PLACES), jnp.int32),
@@ -515,7 +498,6 @@
             pltpu.VMEM((PLACES, CX, CX), F32),
             pltpu.VMEM(tiles, F32),
             dma((16,)),
-            dma((4, PLACES)),
             pltpu.VMEM((TILE * 8 + 8, TILE), F32),
             pltpu.VMEM((TILE * 8, TILE), F32),
             pltpu.VMEM((TILE * 8, TILE), F32),
@@ -542,7 +524,6 @@
             pltpu.VMEM((SLICES, 16, TILE), F32),
             pltpu.VMEM((SLICES, CX, TILE), F32),
             pltpu.VMEM((PLACES, CX, TILE), F32),
-            pltpu.VMEM((PLACES, CX, TILE), F32),
             dma((2,)),
             dma((2,)),
             dma((2, PLACES)),
@@ -553,20 +534,19 @@
             dma((PLACES,)),
         ],
         compiler_params=pltpu.CompilerParams(
-            collective_id=0, has_side_effects=True, vmem_limit_bytes=60 << 20
+            collective_id=0, has_side_effects=True, vmem_limit_bytes=32 << 20
         ),
-    )(substep_scale, neighbors, starts, diffusivity, velocity, obstacle, coarse_x, coarse_y)
+    )(*map(in_hbm, (substep_scale, neighbors, starts, diffusivity, velocity, obstacle, coarse_x, coarse_y)))
     ends, step = pl.pallas_call(
         finish_kernel,
         out_shape=(jax.ShapeDtypeStruct(tiles, F32),) * 2,
-        in_specs=[anywhere] * 6,
+        in_specs=[anywhere] * 2 + [vmem] * 4,
         out_specs=(anywhere, anywhere),
         scratch_shapes=[pltpu.SMEM((4, PLACES), jnp.int32), pltpu.VMEM(tiles, F32)]
-        + [pltpu.VMEM((PLACES, CX, TILE), F32)] * 4
         + [pltpu.VMEM(tiles, F32)] * 2
-        + [dma((6,)), dma((2, PLACES))],
-        compiler_params=pltpu.CompilerParams(vmem_limit_bytes=60 << 20),
-    )(neighbors, starts, sums, coarse, half, prev)
+        + [dma((2,)), dma((2, PLACES))],
+        compiler_params=pltpu.CompilerParams(vmem_limit_bytes=32 << 20),
+    )(in_hbm(neighbors), in_hbm(starts), sums, coarse, half, prev)
     return ends[None], step[None]
 
 

time: 34.8 us -> 33.4 us (0.960)
  Pallas kernels: 34.1 us -> 32.7 us
    pallas_call x1, Pallas kernels: 31.7 us -> 30.7 us  [on_device(): pl.pallas_call(fine_kernel, out_shape=(places,) * 4, in_specs=[anywhere]...]
    pallas_call x1, Pallas kernels: 2.35 us -> 1.99 us  [on_device(): pl.pallas_call(finish_kernel, out_shape=(jax.ShapeDtypeStruct(tiles, F32)...]
where the time goes in v4:
time: 33.4 us; the launch traced here: 33.3 us
  Pallas kernels  32.7 us (98%)
  between operations  0.64 us (2%)
    pallas_call x1, Pallas kernels, on_device(): pl.pallas_call(fine_kernel, out_shape=(places,) * 4, in_specs=[anywhere]...  30.7 us
    pallas_call x1, Pallas kernels, on_device(): pl.pallas_call(finish_kernel, out_shape=(jax.ShapeDtypeStruct(tiles, F32)...  1.99 us

profile of v4, /device:TPU:27, one launch (start us, length us, event | category | flops | bytes accessed | tf_op | source)
XLA Modules:
  0.0 33.3 jit_solution(14780700508508942360)
XLA Ops:
  0.6 30.7 %shard_map.95 = (f32[8,64,128]{2,1,0:T(8,128)S(1)}, f32[8,64,128]{2,1,0:T(8,128)S(1)}, f32[8,64,128]{2,1,0:T(8,128)S(1)}, f32[8,64,128]{2,1,0:T(8,128)S(1)}) custom-call(f32[12]{0:T(128)} %scale_hbm.1, s32[4,8]{1,0:T(4,128)} %bitcast.6, f32[8,128,128]{2,1,0:T(8,128)} %bitcast.4, f32[8,128,128]{2,1,0:T(8,128)} %diff_hbm.1, f32[2,8,128,128]{3,2,1,0:T(8,128)} %vel_hbm.1, ...), custom_call_target="tpu_custom_call" | custom-call | tf_op jit(solution)/shard_map/pallas_call | solution.py:482
  31.3 2.0 %shard_map.96 = (f32[8,128,128]{2,1,0:T(8,128)}, f32[8,128,128]{2,1,0:T(8,128)}) custom-call(s32[4,8]{1,0:T(4,128)} %bitcast.7, f32[8,128,128]{2,1,0:T(8,128)} %bitcast.5, f32[8,64,128]{2,1,0:T(8,128)S(1)} %get-tuple-element.8.sums, f32[8,64,128]{2,1,0:T(8,128)S(1)} %get-tuple-element.9.coarse, f32[8,64,128]{2,1,0:T(8,128)S(1)} %get-tuple-element.10.half, ...), custom_call_target="tpu_custom_call" | custom-call | tf_op jit(solution)/shard_map/pallas_call | solution.py:540

commit v5 on v4

--- a/solution.py
+++ b/solution.py
@@ -42,13 +42,13 @@
 
 def fine_kernel(
     scale_hbm, neighbors_hbm, starts_hbm, diff_hbm, vel_hbm, obst_hbm, cx_hbm, cy_hbm,
-    sum_out, coarse_out, half_out, prev_out,
+    sum_out, coarse_out, half_out, even_out, odd_out,
     scale, neighbors, starts_edge, diff_edge, vel_edge, obst_edge, starts, diff, vel, obst,
     cx, cy, load_sem,
     state, coef_d, coef_a, coef_b, west, east, west_past, east_past,
     xh, xl, yh, yl, coarse_starts, coarse_ends, mean, half,
     jump_mid, jump_edge, half_mid, half_edge, prev_mid, prev_edge, jumps_mid, jumps_edge,
-    chain, coarse,
+    chain, coarse, mean_place,
     halo_ss, halo_rs, jump_ss, jump_rs, half_ss, half_rs, chain_ss, chain_rs,
 ):
     tm = lax.axis_index("tm")
@@ -388,26 +388,44 @@
     def _():
         coarse[...] = coarse_starts[...]
 
-    for p in range(PLACES):
-        half_out[p] = half[pl.ds(p * CX, CX), :]
+    place_of = [
+        jnp.clip(sum(jnp.where(order[p] == t, p, 0) for p in range(PLACES)), 0, PLACES - 1)
+        for t in range(PLACES)
+    ]
+
+    for p in range(PLACES):
+        mean_place[p] = mean[pl.ds(p * CX, CX), :]
+
+    for t in range(PLACES):
+        at = place_of[t]
+        half_out[t, 0:8] = half_edge[at, 0:8]
+        half_out[t, 8 : CX - 8] = half_mid[at]
+        half_out[t, CX - 8 : CX] = half_edge[at, 8:16]
+
+    @pl.when(tm > 0)
+    def _():
+        for copy in half_copies:
+            copy.wait_recv()
+        for t in range(PLACES):
+            at = place_of[t]
+            for rows, difference, first, begin in (
+                (slice(0, 8), prev_edge[at, 0:8], starts_edge, 0),
+                (slice(8, CX - 8), prev_mid[at], starts, 0),
+                (slice(CX - 8, CX), prev_edge[at, 8:16], starts_edge, 16),
+            ):
+                count = rows.stop - rows.start
+                even_out[t, rows] = difference - first[t, pl.ds(begin, count, stride=2), :]
+                odd_out[t, rows] = -difference - first[t, pl.ds(begin + 1, count, stride=2), :]
 
     for p in range(PLACES):
         @pl.when(jnp.logical_and(tm > 0, tm != 2 * p))
         def _(p=p):
             state_arrival(p).wait_recv()
 
-        values = coarse[p]
-        coarse_out[p] = values
-        sum_out[p] = apply_coarse(p, values) + mean[pl.ds(p * CX, CX), :]
-
-    @pl.when(tm > 0)
-    def _():
-        for copy in half_copies:
-            copy.wait_recv()
-        for p in range(PLACES):
-            prev_out[p, 0:8] = prev_edge[p, 0:8]
-            prev_out[p, 8 : CX - 8] = prev_mid[p]
-            prev_out[p, CX - 8 : CX] = prev_edge[p, 8:16]
+    for t in range(PLACES):
+        values = coarse[place_of[t]]
+        coarse_out[t] = values
+        sum_out[t] = apply_coarse(place_of[t], values) + mean_place[place_of[t]]
 
     for p in range(PLACES):
         @pl.when(sends_to(p))
@@ -433,36 +451,20 @@
 
 
 def finish_kernel(
-    neighbors_hbm, starts_hbm, sums, coarse, half, prev, ends_hbm, step_hbm,
-    neighbors, starts, ends, step, load_sem, store_sem,
+    sums, coarse, half, even_part, odd_part, ends_hbm, step_hbm, ends, step, store_sem
 ):
-    loads = [
-        pltpu.make_async_copy(src, dst, load_sem.at[i])
-        for i, (src, dst) in enumerate(
-            [(neighbors_hbm, neighbors), (starts_hbm, starts)]
-        )
-    ]
-    for load in loads:
-        load.start()
     later = lax.axis_index("tm") > 0
     even, odd = pl.ds(0, CX, stride=2), pl.ds(1, CX, stride=2)
-    loads[0].wait()
-    order = place_order(neighbors, lax.axis_index("space"))
     stores = []
-    for p in range(PLACES):
-        t = order[p]
-        total, difference = sums[p], half[p]
-        ends[p, even, :] = total + difference
-        ends[p, odd, :] = total - difference
-        stores.append(pltpu.make_async_copy(ends.at[p], ends_hbm.at[t], store_sem.at[0, p]))
+    for t in range(PLACES):
+        total, difference = sums[t], half[t]
+        ends[t, even, :] = total + difference
+        ends[t, odd, :] = total - difference
+        stores.append(pltpu.make_async_copy(ends.at[t], ends_hbm.at[t], store_sem.at[0, t]))
         stores[-1].start()
-    loads[1].wait()
-    for p in range(PLACES):
-        t = order[p]
-        total, difference = coarse[p], prev[p]
-        step[p, even, :] = jnp.where(later, total + difference - starts[t, even, :], 0.0)
-        step[p, odd, :] = jnp.where(later, total - difference - starts[t, odd, :], 0.0)
-        stores.append(pltpu.make_async_copy(step.at[p], step_hbm.at[t], store_sem.at[1, p]))
+        step[t, even, :] = jnp.where(later, coarse[t] + even_part[t], 0.0)
+        step[t, odd, :] = jnp.where(later, coarse[t] + odd_part[t], 0.0)
+        stores.append(pltpu.make_async_copy(step.at[t], step_hbm.at[t], store_sem.at[1, t]))
         stores[-1].start()
     for store in stores:
         store.wait()
@@ -479,11 +481,11 @@
     starts = starts[0]
     in_hbm = lambda x: pltpu.with_memory_space_constraint(x, pltpu.HBM)
     neighbors = neighbors.T
-    sums, coarse, half, prev = pl.pallas_call(
+    parts = pl.pallas_call(
         fine_kernel,
-        out_shape=(places,) * 4,
+        out_shape=(places,) * 5,
         in_specs=[anywhere] * 8,
-        out_specs=(vmem,) * 4,
+        out_specs=(vmem,) * 5,
         scratch_shapes=[
             pltpu.SMEM((SUB,), F32),
             pltpu.SMEM((4, PLACES), jnp.int32),
@@ -524,6 +526,7 @@
             pltpu.VMEM((SLICES, 16, TILE), F32),
             pltpu.VMEM((SLICES, CX, TILE), F32),
             pltpu.VMEM((PLACES, CX, TILE), F32),
+            pltpu.VMEM((PLACES, CX, TILE), F32),
             dma((2,)),
             dma((2,)),
             dma((2, PLACES)),
@@ -540,13 +543,11 @@
     ends, step = pl.pallas_call(
         finish_kernel,
         out_shape=(jax.ShapeDtypeStruct(tiles, F32),) * 2,
-        in_specs=[anywhere] * 2 + [vmem] * 4,
+        in_specs=[vmem] * 5,
         out_specs=(anywhere, anywhere),
-        scratch_shapes=[pltpu.SMEM((4, PLACES), jnp.int32), pltpu.VMEM(tiles, F32)]
-        + [pltpu.VMEM(tiles, F32)] * 2
-        + [dma((2,)), dma((2, PLACES))],
+        scratch_shapes=[pltpu.VMEM(tiles, F32)] * 2 + [dma((2, PLACES))],
         compiler_params=pltpu.CompilerParams(vmem_limit_bytes=32 << 20),
-    )(in_hbm(neighbors), in_hbm(starts), sums, coarse, half, prev)
+    )(*parts)
     return ends[None], step[None]
 
 

time: 33.4 us -> 31.9 us (0.955)
  Pallas kernels: 32.7 us -> 31.1 us
    pallas_call x1, Pallas kernels: 1.99 us -> 1.1 us  [on_device(): pl.pallas_call(finish_kernel, out_shape=(jax.ShapeDtypeStruct(tiles, F32)...]
    pallas_call x1, Pallas kernels: 30.7 us -> 30 us  [on_device(): pl.pallas_call(fine_kernel, out_shape=(places,) * 5, in_specs=[anywhere]...]
where the time goes in v5:
time: 31.9 us; the launch traced here: 31.7 us
  Pallas kernels  31.1 us (97%)
  between operations  0.64 us (2%)
    pallas_call x1, Pallas kernels, on_device(): pl.pallas_call(fine_kernel, out_shape=(places,) * 5, in_specs=[anywhere]...  30 us
    pallas_call x1, Pallas kernels, on_device(): pl.pallas_call(finish_kernel, out_shape=(jax.ShapeDtypeStruct(tiles, F32)...  1.1 us

profile of v5, /device:TPU:27, one launch (start us, length us, event | category | flops | bytes accessed | tf_op | source)
XLA Modules:
  0.0 31.7 jit_solution(10046235861435128379)
XLA Ops:
  0.6 30.0 %shard_map.95 = (f32[8,64,128]{2,1,0:T(8,128)S(1)}, f32[8,64,128]{2,1,0:T(8,128)S(1)}, f32[8,64,128]{2,1,0:T(8,128)S(1)}, f32[8,64,128]{2,1,0:T(8,128)S(1)}, f32[8,64,128]{2,1,0:T(8,128)S(1)}) custom-call(f32[12]{0:T(128)} %scale_hbm.1, s32[4,8]{1,0:T(4,128)} %bitcast.5, f32[8,128,128]{2,1,0:T(8,128)} %bitcast.4, f32[8,128,128]{2,1,0:T(8,128)} %diff_hbm.1, ...), custom_call_target="tpu_custom_call" | custom-call | tf_op jit(solution)/shard_map/pallas_call | solution.py:484
  30.6 1.1 %shard_map.96 = (f32[8,128,128]{2,1,0:T(8,128)}, f32[8,128,128]{2,1,0:T(8,128)}) custom-call(f32[8,64,128]{2,1,0:T(8,128)S(1)} %get-tuple-element.9.sums, f32[8,64,128]{2,1,0:T(8,128)S(1)} %get-tuple-element.10.coarse, f32[8,64,128]{2,1,0:T(8,128)S(1)} %get-tuple-element.11.half, f32[8,64,128]{2,1,0:T(8,128)S(1)} %get-tuple-element.12.even_part, ...), custom_call_target="tpu_custom_call" | custom-call | tf_op jit(solution)/shard_map/pallas_call | solution.py:543
